TPU v7x, 32 devices: a whole 2x2x4 slice. The times are simulated.
32 devices in a mesh: dp: 8 (over z, x), fsdp: 4 (over y, core).
Axes of the slice: x: 2, y: 2, z: 4, core: 2. Of those that a mesh axis runs over, the one named last changes fastest.
Arguments:
- block_in: bfloat16 [160, 185, 768], P(('dp', 'fsdp')), may hold values from -6 to 6
- out_grad: bfloat16 [160, 185, 768], P(('dp', 'fsdp')), may hold values from -8 to 8
- caption_len: int32 [160], P(('dp', 'fsdp')), may hold values from 4 to 40, as said below
- mask_marks: int32 [160, 40], P(('dp', 'fsdp')), may hold values 0 or 1
- qkv_weight: float32 [768, 2304], P('fsdp'), may hold values from -0.21875 to 0.21875
- out_weight: float32 [768, 768], P(None, 'fsdp'), may hold values from -1.75 to 1.75
- up_weight: float32 [768, 3072], P('fsdp'), may hold values from -0.21875 to 0.21875
- down_weight: float32 [3072, 768], P(None, 'fsdp'), may hold values from -0.109375 to 0.109375
- vector_params: float32 [13, 768], P(None, 'fsdp'), may hold values from -6 to 6
- qkv_first: float32 [768, 2304], P('fsdp'), may hold values from -688.18604 to 688.18604
- qkv_second: float32 [768, 2304], P('fsdp'), may hold values from 24272 to 97680
- out_first: float32 [768, 768], P(None, 'fsdp'), may hold values from -123.87348 to 123.87348
- out_second: float32 [768, 768], P(None, 'fsdp'), may hold values from 799.2 to 3167.2
- up_first: float32 [768, 3072], P('fsdp'), may hold values from -240.86511 to 240.86511
- up_second: float32 [768, 3072], P('fsdp'), may hold values from 2960 to 11840
- down_first: float32 [3072, 768], P(None, 'fsdp'), may hold values from -481.73022 to 481.73022
- down_second: float32 [3072, 768], P(None, 'fsdp'), may hold values from 11840 to 47360
- vector_first: float32 [13, 768], P(None, 'fsdp'), may hold values from -1204.32554 to 1204.32554
- vector_second: float32 [13, 768], P(None, 'fsdp'), may hold values from 888 to 296000
Outputs:
- block_out: bfloat16 [160, 185, 768], P(('dp', 'fsdp'))
- input_grad: float32 [160, 185, 768], P(('dp', 'fsdp'))
- qkv_new: float32 [768, 2304], P('fsdp')
- out_new: float32 [768, 768], P(None, 'fsdp')
- up_new: float32 [768, 3072], P('fsdp')
- down_new: float32 [3072, 768], P(None, 'fsdp')
- vector_new: float32 [13, 768], P(None, 'fsdp')
- qkv_first_new: float32 [768, 2304], P('fsdp')
- qkv_second_new: float32 [768, 2304], P('fsdp')
- out_first_new: float32 [768, 768], P(None, 'fsdp')
- out_second_new: float32 [768, 768], P(None, 'fsdp')
- up_first_new: float32 [768, 3072], P('fsdp')
- up_second_new: float32 [768, 3072], P('fsdp')
- down_first_new: float32 [3072, 768], P(None, 'fsdp')
- down_second_new: float32 [3072, 768], P(None, 'fsdp')
- vector_first_new: float32 [13, 768], P(None, 'fsdp')
- vector_second_new: float32 [13, 768], P(None, 'fsdp')
- matrix_norms: float32 [2, 4], replicated
Inputs may be any that keep to these rules, and one draw needn't show every extreme that they name: `caption_len`: caption positions from an item's length on are padding; on every device of dp+fsdp one of its 5 items has the full 40.
All inputs are finite; a program needn't handle non-finite values. No bound on the sum of `mask_marks` on one device may be relied on, other than what follows from the above.
Results may differ from a plain program's by a relative error of at most 0.018.
The roundings to bfloat16 on the way count: a program that leaves them out, or rounds other values in their place, can miss the bound.
Values may be sent and summed in bfloat16 or wider, within the bound.
No kernel may reach another device: no remote copies, remote signals or barrier semaphores. Data moves between devices by JAX's collectives and lax.ppermute only.
A program may use at most 192 MiB of HBM per device.

v0:
```python
import jax
import jax.numpy as jnp
from jax import lax
from jax.sharding import PartitionSpec as P

HEAD = 64
TXT = 40
PATCH = 145
STEP = 7


ln_eps = 1e-06
beta_one = 0.5
beta_two = 0.55
adam_eps = 1e-06
decay_rate = 0.01
matrix_rate = 0.5
vector_rate = 0.3


def masks_for(lengths, marks):
    places = jnp.arange(TXT + PATCH, dtype=jnp.int32)
    key_valid = (places[None, :] >= TXT) | (places[None, :] < lengths[:, None])
    text_places = jnp.arange(TXT, dtype=jnp.int32)
    live = (marks == 1) & (text_places[None, :] >= 1) & (text_places[None, :] < lengths[:, None])
    chosen = jnp.concatenate([live, jnp.zeros((lengths.shape[0], PATCH), dtype=bool)], axis=1)
    return (key_valid, chosen)


def normalize(rows, gain, shift):
    centred = rows - jnp.mean(rows, axis=-1, keepdims=True)
    factor = lax.rsqrt(jnp.mean(centred * centred, axis=-1, keepdims=True) + ln_eps)
    unit = centred * factor
    return (unit * gain + shift, unit, factor)


def normalize_back(grad_normed, unit, factor, gain):
    grad_unit = grad_normed * gain
    grad_rows = factor * (
        grad_unit
        - jnp.mean(grad_unit, axis=-1, keepdims=True)
        - unit * jnp.mean(grad_unit * unit, axis=-1, keepdims=True)
    )
    return (grad_rows, jnp.sum(grad_normed * unit, axis=0), jnp.sum(grad_normed, axis=0))


def gelu_slope(values_in):
    normal_cdf = 0.5 * (1.0 + lax.erf(values_in * 0.7071067811865476))
    return normal_cdf + values_in * jnp.exp(-0.5 * values_in * values_in) * 0.3989422804014327


def run_forward(inputs, key_valid, chosen, params):
    qkv_weight, out_weight, up_weight, down_weight, vectors = params
    vector_rows = vectors.astype(jnp.float32)
    n_items, seq_len, width = inputs.shape
    heads = width // HEAD
    start = jnp.where(
        chosen[:, :, None], vector_rows[12][None, None, :], inputs.astype(jnp.float32)
    )
    flat = start.reshape(n_items * seq_len, width)
    normed, unit_one, factor_one = normalize(flat, vector_rows[0], vector_rows[1])
    normed_low = normed.astype(jnp.bfloat16)
    mixed_bias = jnp.concatenate([vector_rows[2], jnp.zeros_like(vector_rows[2]), vector_rows[3]])
    mixed = jnp.dot(normed_low, qkv_weight, preferred_element_type=jnp.float32) + mixed_bias
    mixed_low = mixed.astype(jnp.bfloat16).reshape(n_items, seq_len, 3, heads, HEAD)
    queries = mixed_low[:, :, 0]
    keys_low = mixed_low[:, :, 1]
    values_low = mixed_low[:, :, 2]
    scores = jnp.einsum(
        "nqhe,nkhe->nhqk", queries, keys_low, preferred_element_type=jnp.float32
    ) * HEAD ** (-0.5)
    scores = jnp.where(key_valid[:, None, None, :], scores, -1000000000.0)
    shifted = scores - jnp.max(scores, axis=-1, keepdims=True)
    expd = jnp.exp(shifted)
    probs = expd / jnp.sum(expd, axis=-1, keepdims=True)
    probs_low = probs.astype(jnp.bfloat16)
    attended = jnp.einsum(
        "nhqk,nkhe->nqhe", probs_low, values_low, preferred_element_type=jnp.float32
    )
    attended_low = attended.astype(jnp.bfloat16).reshape(n_items * seq_len, width)
    middle = (
        flat
        + jnp.dot(attended_low, out_weight, preferred_element_type=jnp.float32)
        + vector_rows[4]
    )
    normed_two, unit_two, factor_two = normalize(middle, vector_rows[5], vector_rows[6])
    normed_two_low = normed_two.astype(jnp.bfloat16)
    hidden = jnp.dot(normed_two_low, up_weight, preferred_element_type=jnp.float32) + vector_rows[
        8:12
    ].reshape(-1)
    activated_low = jax.nn.gelu(hidden, approximate=False).astype(jnp.bfloat16)
    result = (
        middle
        + jnp.dot(activated_low, down_weight, preferred_element_type=jnp.float32)
        + vector_rows[7]
    )
    kept = (
        normed_low,
        unit_one,
        factor_one,
        queries,
        keys_low,
        values_low,
        probs,
        probs_low,
        attended_low,
        unit_two,
        factor_two,
        normed_two_low,
        hidden,
        activated_low,
    )
    return (result.reshape(n_items, seq_len, width), kept)


def run_backward(kept, out_grad, params, chosen):
    qkv_weight, out_weight, up_weight, down_weight, vectors = params
    vector_rows = vectors.astype(jnp.float32)
    (
        normed_low,
        unit_one,
        factor_one,
        queries,
        keys_low,
        values_low,
        probs,
        probs_low,
        attended_low,
        unit_two,
        factor_two,
        normed_two_low,
        hidden,
        activated_low,
    ) = kept
    n_items, seq_len, width = out_grad.shape
    heads = width // HEAD
    row_count = n_items * seq_len
    grad_top = out_grad.astype(jnp.float32).reshape(row_count, width)
    grad_branch_two = grad_top.astype(jnp.bfloat16)
    grad_down = jnp.einsum(
        "rf,rd->fd", activated_low, grad_branch_two, preferred_element_type=jnp.float32
    )
    bias_down = jnp.sum(grad_branch_two.astype(jnp.float32), axis=0)
    grad_activated = jnp.einsum(
        "rd,fd->rf", grad_branch_two, down_weight, preferred_element_type=jnp.float32
    )
    grad_hidden = (grad_activated * gelu_slope(hidden)).astype(jnp.bfloat16)
    grad_up = jnp.einsum(
        "rd,rf->df", normed_two_low, grad_hidden, preferred_element_type=jnp.float32
    )
    bias_up = jnp.sum(grad_hidden.astype(jnp.float32), axis=0)
    grad_normed_two = jnp.einsum(
        "rf,df->rd", grad_hidden, up_weight, preferred_element_type=jnp.float32
    )
    grad_middle_norm, gain_two, shift_two = normalize_back(
        grad_normed_two, unit_two, factor_two, vector_rows[5]
    )
    grad_middle = grad_top + grad_middle_norm
    grad_branch_one = grad_middle.astype(jnp.bfloat16)
    grad_outer = jnp.einsum(
        "rd,re->de", attended_low, grad_branch_one, preferred_element_type=jnp.float32
    )
    bias_outer = jnp.sum(grad_branch_one.astype(jnp.float32), axis=0)
    grad_attended = jnp.einsum(
        "re,de->rd", grad_branch_one, out_weight, preferred_element_type=jnp.float32
    )
    grad_attended = grad_attended.astype(jnp.bfloat16).reshape(n_items, seq_len, heads, HEAD)
    grad_values = jnp.einsum(
        "nhqk,nqhe->nkhe", probs_low, grad_attended, preferred_element_type=jnp.float32
    ).astype(jnp.bfloat16)
    grad_probs = jnp.einsum(
        "nqhe,nkhe->nhqk", grad_attended, values_low, preferred_element_type=jnp.float32
    )
    grad_scores = (
        probs * (grad_probs - jnp.sum(grad_probs * probs, axis=-1, keepdims=True))
    ).astype(jnp.bfloat16)
    grad_queries = (
        jnp.einsum("nhqk,nkhe->nqhe", grad_scores, keys_low, preferred_element_type=jnp.float32)
        * HEAD ** (-0.5)
    ).astype(jnp.bfloat16)
    grad_keys = (
        jnp.einsum("nhqk,nqhe->nkhe", grad_scores, queries, preferred_element_type=jnp.float32)
        * HEAD ** (-0.5)
    ).astype(jnp.bfloat16)
    grad_mixed = jnp.stack([grad_queries, grad_keys, grad_values], axis=2).reshape(
        row_count, 3 * width
    )
    grad_qkv = jnp.einsum("rd,rc->dc", normed_low, grad_mixed, preferred_element_type=jnp.float32)
    bias_mixed = jnp.sum(grad_mixed.astype(jnp.float32), axis=0)
    grad_normed = jnp.einsum(
        "rc,dc->rd", grad_mixed, qkv_weight, preferred_element_type=jnp.float32
    )
    grad_start_norm, gain_one, shift_one = normalize_back(
        grad_normed, unit_one, factor_one, vector_rows[0]
    )
    grad_start = (grad_middle + grad_start_norm).reshape(n_items, seq_len, width)
    marked = chosen[:, :, None]
    grad_embed = jnp.sum(jnp.where(marked, grad_start, 0.0), axis=(0, 1))
    input_grad = jnp.where(marked, 0.0, grad_start)
    head_rows = jnp.stack(
        [
            gain_one,
            shift_one,
            bias_mixed[:width],
            bias_mixed[2 * width :],
            bias_outer,
            gain_two,
            shift_two,
            bias_down,
        ]
    )
    grad_vectors = jnp.concatenate(
        [head_rows, bias_up.reshape(4, width), grad_embed[None, :]], axis=0
    )
    return ((grad_qkv, grad_outer, grad_up, grad_down, grad_vectors), input_grad)


def adam_moments(grad, first, second):
    first_new = beta_one * first + (1.0 - beta_one) * grad
    second_new = beta_two * second + (1.0 - beta_two) * grad * grad
    direction = (
        first_new
        / (1.0 - beta_one**STEP)
        / (jnp.sqrt(second_new / (1.0 - beta_two**STEP)) + adam_eps)
    )
    return (first_new, second_new, direction)


def local(
    block_in,
    out_grad,
    caption_len,
    mask_marks,
    qkv_weight,
    out_weight,
    up_weight,
    down_weight,
    vector_params,
    qkv_first,
    qkv_second,
    out_first,
    out_second,
    up_first,
    up_second,
    down_first,
    down_second,
    vector_first,
    vector_second,
):
    key_valid, chosen = masks_for(caption_len, mask_marks)
    masters = (qkv_weight, out_weight, up_weight, down_weight)
    qkv_low = qkv_weight.astype(jnp.bfloat16)
    out_low = out_weight.astype(jnp.bfloat16)
    up_low = up_weight.astype(jnp.bfloat16)
    down_low = down_weight.astype(jnp.bfloat16)
    vector_low = vector_params.astype(jnp.bfloat16)
    shared = (
        lax.all_gather(qkv_low, "fsdp", axis=0, tiled=True),
        lax.all_gather(out_low, "fsdp", axis=1, tiled=True),
        lax.all_gather(up_low, "fsdp", axis=0, tiled=True),
        lax.all_gather(down_low, "fsdp", axis=1, tiled=True),
        lax.all_gather(vector_low, "fsdp", axis=1, tiled=True),
    )
    result, unused = run_forward(block_in, key_valid, chosen, shared)
    block_out = result.astype(jnp.bfloat16)
    again = (
        lax.all_gather(qkv_low, "fsdp", axis=0, tiled=True),
        lax.all_gather(out_low, "fsdp", axis=1, tiled=True),
        lax.all_gather(up_low, "fsdp", axis=0, tiled=True),
        lax.all_gather(down_low, "fsdp", axis=1, tiled=True),
        lax.all_gather(vector_low, "fsdp", axis=1, tiled=True),
    )
    redone, kept = run_forward(block_in, key_valid, chosen, again)
    grads, input_grad = run_backward(kept, out_grad, again, chosen)
    own_squares = jnp.stack([jnp.sum(master * master) for master in masters])
    summed = (
        lax.psum_scatter(
            grads[0].astype(jnp.bfloat16), "fsdp", scatter_dimension=0, tiled=True
        ).astype(jnp.float32),
        lax.psum_scatter(
            grads[1].astype(jnp.bfloat16), "fsdp", scatter_dimension=1, tiled=True
        ).astype(jnp.float32),
        lax.psum_scatter(
            grads[2].astype(jnp.bfloat16), "fsdp", scatter_dimension=0, tiled=True
        ).astype(jnp.float32),
        lax.psum_scatter(
            grads[3].astype(jnp.bfloat16), "fsdp", scatter_dimension=1, tiled=True
        ).astype(jnp.float32),
        lax.psum_scatter(
            grads[4].astype(jnp.bfloat16), "fsdp", scatter_dimension=1, tiled=True
        ).astype(jnp.float32),
    )
    reduced = lax.psum((summed[0], summed[1], summed[2], summed[3], summed[4]), "dp")
    firsts = (qkv_first, out_first, up_first, down_first, vector_first)
    seconds = (qkv_second, out_second, up_second, down_second, vector_second)
    moved = [adam_moments(reduced[index], firsts[index], seconds[index]) for index in range(5)]
    updates = [moved[index][2] + decay_rate * masters[index] for index in range(4)]
    update_squares = jnp.stack([jnp.sum(update * update) for update in updates])
    weight_squares, update_squares = lax.psum((own_squares, update_squares), "fsdp")
    ratios = jnp.sqrt(weight_squares) * lax.rsqrt(update_squares + adam_eps)
    new_weights = [
        masters[index] - matrix_rate * ratios[index] * updates[index] for index in range(4)
    ]
    vector_new = vector_params - vector_rate * moved[4][2]
    matrix_norms = jnp.stack([jnp.sqrt(weight_squares), jnp.sqrt(update_squares)])
    return (
        block_out,
        input_grad,
        new_weights[0],
        new_weights[1],
        new_weights[2],
        new_weights[3],
        vector_new,
        moved[0][0],
        moved[0][1],
        moved[1][0],
        moved[1][1],
        moved[2][0],
        moved[2][1],
        moved[3][0],
        moved[3][1],
        moved[4][0],
        moved[4][1],
        matrix_norms,
    )


def solution(mesh):
    placed = (
        P(("dp", "fsdp"), None, None),
        P(("dp", "fsdp"), None, None),
        P(("dp", "fsdp")),
        P(("dp", "fsdp"), None),
        P("fsdp", None),
        P(None, "fsdp"),
        P("fsdp", None),
        P(None, "fsdp"),
        P(None, "fsdp"),
        P("fsdp", None),
        P("fsdp", None),
        P(None, "fsdp"),
        P(None, "fsdp"),
        P("fsdp", None),
        P("fsdp", None),
        P(None, "fsdp"),
        P(None, "fsdp"),
        P(None, "fsdp"),
        P(None, "fsdp"),
    )
    return jax.shard_map(
        local,
        mesh=mesh,
        in_specs=placed,
        out_specs=(
            P(("dp", "fsdp"), None, None),
            P(("dp", "fsdp"), None, None),
            P("fsdp", None),
            P(None, "fsdp"),
            P("fsdp", None),
            P(None, "fsdp"),
            P(None, "fsdp"),
            P("fsdp", None),
            P("fsdp", None),
            P(None, "fsdp"),
            P(None, "fsdp"),
            P("fsdp", None),
            P("fsdp", None),
            P(None, "fsdp"),
            P(None, "fsdp"),
            P(None, "fsdp"),
            P(None, "fsdp"),
            P(),
        ),
        check_vma=False,
    )
```

profile of v0, /device:TPU:0, one launch (start us, length us, event | category | flops | bytes accessed | tf_op | source)
XLA Modules:
  0.0 796.8 jit_solution(12410185632766353821)
XLA Ops:
  7.2 2.5 convert_element_type.143
  10.7 2.8 convert_element_type.150
  14.9 6.3 all-gather
  28.5 2.5 add_convert_fusion.1
  31.0 2.3 reshape.206
  33.4 10.3 %all-gather.6.cloned.1.call-done = bf16[768,2304]{1,0:T(8,128)(2,1)} async-done(((bf16[192,2304]{1,0:T(8,128)(2,1)}), bf16[768,2304]{1,0:T(8,128)(2,1)}) %all-gather.6.cloned.1.call-update) | async-done | bytes 3538960 | tf_op jit(solution)/shard_map/all_gather | solution.py:258
  43.7 7.4 add_convert_fusion
  51.0 13.9 %reshape.219 = bf16[5,185,3,12,64]{4,3,2,1,0:T(8,128)(2,1)} reshape(bf16[925,2304]{1,0:T(8,128)(2,1)} %add_convert_fusion) | data formatting | bytes 8524800 | tf_op jit(solution)/shard_map/reshape | solution.py:65
  64.9 8.6 %fusion.70 = (bf16[5,185,1,12,64]{4,3,2,1,0:T(8,128)(2,1)}, bf16[5,185,1,12,64]{4,3,2,1,0:T(8,128)(2,1)}, bf16[5,185,1,12,64]{4,3,2,1,0:T(8,128)(2,1)}) fusion(bf16[5,185,3,12,64]{4,3,2,1,0:T(8,128)(2,1)} %reshape.219), kind=kLoop, calls=%fused_computation.158 | loop fusion | bytes 8524800 | tf_op jit(solution)/shard_map/slice | solution.py:66
  73.6 5.9 copy.85
  79.5 5.9 copy.84
  85.4 5.4 copy.86
  90.8 8.3 %fusion.28 = f32[5,12,185,185]{2,3,1,0:T(8,128)} fusion(bf16[5,185,1,12,64]{1,4,3,0,2:T(8,128)(2,1)S(1)} %copy.86, bf16[5,185,1,12,64]{1,4,3,0,2:T(8,128)(2,1)} %copy.85), kind=kOutput, calls=%fused_computation.80 | convolution fusion | flops 262848000 | bytes 11055600 | tf_op jit(solution)/shard_map/nqhe,nkhe->nhqk/dot_general | solution.py:69
  99.1 17.5 %fusion.73 = (f32[5,12,185]{2,1,0:T(8,128)S(1)}, f32[5,12,185,185]{2,3,1,0:T(8,128)}) fusion(f32[5,12,185,185]{2,3,1,0:T(8,128)} %fusion.28, pred[5,185]{1,0:T(8,128)(4,1)S(1)} %fusion.57), kind=kOutput, calls=%fused_computation.161 | output fusion | flops 12321184 | bytes 16473325 | tf_op jit(solution)/shard_map/sub | solution.py:73
  116.6 5.6 convert_bitcast_fusion.1
  123.7 3.5 reshape.208
  127.1 4.2 fusion.74
  133.6 34.1 %fusion.3 = (bf16[925,3072]{1,0:T(8,128)(2,1)}, f32[925,3072]{1,0:T(8,128)}) fusion(f32[3072]{0:T(1024)S(1)} %add.240, bf16[768,3072]{1,0:T(8,128)(2,1)} %all-gather.10.cloned.1.call-done, f32[925,768]{1,0:T(8,128)} %copy-done.12, f32[768]{0:T(1024)S(1)} %get-tuple-element.27, f32[768]{0:T(1024)S(1)} %get-tuple-element.28, f32[925]{0:T(1024)S(1)} %add_rsqrt_fusion.1, ...), kind=kOutput, calls=%fused_computation.9 | convolution fusion | flops 4555795456 | bytes 24635624 | tf_op jit(solution)/shard_map/dot_general | solution.py:88
  167.7 11.2 %fusion.75 = (bf16[3072]{0:T(1024)(128)(2,1)S(1)}, bf16[925,3072]{1,0:T(8,128)(2,1)S(1)}) fusion(f32[925,3072]{1,0:T(8,128)} %get-tuple-element.90, f32[3072]{0:T(1024)S(1)} %add.240, bf16[3072,768]{0,1:T(8,128)(2,1)} %all-gather.12.cloned.1.call-done, f32[925,768]{1,0:T(8,128)S(1)} %copy-done.10), kind=kOutput, calls=%fused_computation.163 | convolution fusion | flops 4399504384 | bytes 24628224 | tf_op jit(solution)/shard_map/rd,fd->rf/dot_general | solution.py:144
  179.0 5.2 multiply_reduce_fusion.2
  188.2 4.2 reshape.220
  192.4 6.1 copy.68
  198.4 8.4 %convert_bitcast_fusion = bf16[5,185,1,12,64]{1,4,3,0,2:T(8,128)(2,1)} fusion(bf16[5,185,12,64]{1,3,2,0:T(8,128)(2,1)} %copy.68, f32[5,12,185,185]{2,3,1,0:T(8,128)} %get-tuple-element.86, f32[5,12,185]{2,1,0:T(8,128)S(1)} %get-tuple-element.85), kind=kOutput, calls=%fused_computation.87 | convolution fusion | flops 267665408 | bytes 11100000 | tf_op jit(solution)/shard_map/nhqk,nqhe->nkhe/dot_general | solution.py:168
  207.6 5.6 multiply_reduce_fusion
  213.3 6.7 multiply_convert_fusion
  221.9 2.5 fusion.43
  224.5 5.9 fusion.69
  230.5 11.3 %copy.73 = bf16[5,185,3,12,64]{1,0,4,3,2:T(8,128)(2,1)} copy(bf16[5,185,3,12,64]{1,4,3,0,2:T(8,128)(2,1)} %get-tuple-element.61) | data formatting | bytes 8524800 | tf_op jit(solution)/shard_map/stack | solution.py:185
  241.9 14.0 %reshape.211 = bf16[925,2304]{0,1:T(8,128)(2,1)} reshape(bf16[5,185,3,12,64]{1,0,4,3,2:T(8,128)(2,1)} %copy.73) | data formatting | bytes 8524800 | tf_op jit(solution)/shard_map/reshape | solution.py:185
  256.0 8.6 %multiply_reduce_fusion.3 = (bf16[768]{0:T(1024)(128)(2,1)S(1)}, f32[925]{0:T(1024)S(1)}, f32[925]{0:T(1024)S(1)}, bf16[768]{0:T(1024)(128)(2,1)S(1)}, f32[925,768]{1,0:T(8,128)S(1)}) fusion(f32[925,768]{1,0:T(8,128)S(1)} %copy-done.17, f32[925]{0:T(1024)S(1)} %copy-done.47, f32[925]{0:T(1024)S(1)} %copy-done.45, f32[768]{0:T(1024)S(1)} %copy-done.43, ...), kind=kOutput, calls=%fused_computation.54 | convolution fusion | flops 3279913216 | bytes 13505488 | tf_op jit(solution)/shard_map/rc,dc->rd/dot_general | solution.py:190
  264.6 2.4 select_reduce_fusion
  268.0 4.8 convolution_convert_fusion.4
  273.4 7.9 convolution_convert_fusion.2
  283.0 9.6 %convolution_convert_fusion = bf16[3072,768]{0,1:T(8,128)(2,1)} fusion(bf16[925,3072]{1,0:T(8,128)(2,1)} %get-tuple-element.89, f32[925,768]{1,0:T(8,128)S(1)} %copy-done.11), kind=kOutput, calls=%fused_computation.38 | convolution fusion | flops 4367767552 | bytes 13243392 | tf_op jit(solution)/shard_map/rf,rd->fd/dot_general | solution.py:140
  294.5 9.9 %convolution_convert_fusion.1 = bf16[768,3072]{1,0:T(8,128)(2,1)} fusion(bf16[925,3072]{1,0:T(8,128)(2,1)} %copy-done.57, f32[925,768]{1,0:T(8,128)S(1)} %copy-done.14, f32[768]{0:T(1024)S(1)} %get-tuple-element.27, f32[768]{0:T(1024)S(1)} %get-tuple-element.28, f32[925]{0:T(1024)S(1)} %add_rsqrt_fusion.1, f32[925]{0:T(1024)S(1)} %broadcast_multiply_fusion.10), kind=kOutput, calls=%fused_computation.39 | convolution fusion | flops 4370609152 | bytes 13256936 | tf_op jit(solution)/shard_map/rd,rf->df/dot_general | solution.py:148
  309.5 9.8 %add_convert_fusion.2 = bf16[925,768]{1,0:T(8,128)(2,1)} fusion(f32[925,768]{1,0:T(8,128)S(1)} %copy-done.15, bf16[925,3072]{1,0:T(8,128)(2,1)} %get-tuple-element.89, bf16[3072,768]{0,1:T(8,128)(2,1)} %all-gather.12.cloned.1.call-done, f32[768]{0:T(1024)S(1)} %copy-done.52), kind=kOutput, calls=%fused_computation.59 | convolution fusion | flops 4366829568 | bytes 14667264 | tf_op jit(solution)/shard_map/dot_general | solution.py:94
  320.3 40.1 %reduce-scatter.8.cloned.1.call-done = bf16[192,2304]{1,0:T(8,128)(2,1)} async-done(((bf16[768,2304]{1,0:T(8,128)(2,1)}), bf16[192,2304]{1,0:T(8,128)(2,1)}) %reduce-scatter.8.cloned.1.call-update) | async-done | bytes 884752 | tf_op jit(solution)/shard_map/reduce_scatter | solution.py:277
  360.4 50.4 %reduce-scatter.14.cloned.1.call-done = bf16[3072,192]{0,1:T(8,128)(2,1)} async-done(((bf16[3072,768]{0,1:T(8,128)(2,1)}), bf16[3072,192]{0,1:T(8,128)(2,1)}) %reduce-scatter.14.cloned.1.call-update) | async-done | bytes 1179664 | tf_op jit(solution)/shard_map/reduce_scatter | solution.py:286
  410.8 50.6 %reduce-scatter.12.cloned.1.call-done = bf16[192,3072]{1,0:T(8,128)(2,1)} async-done(((bf16[768,3072]{1,0:T(8,128)(2,1)}), bf16[192,3072]{1,0:T(8,128)(2,1)}) %reduce-scatter.12.cloned.1.call-update) | async-done | bytes 1179664 | tf_op jit(solution)/shard_map/reduce_scatter | solution.py:283
  461.4 279.3 %all-reduce.4 = (f32[192,2304]{1,0:T(8,128)}, f32[3072,192]{0,1:T(8,128)}, f32[192,3072]{1,0:T(8,128)}, f32[768,192]{0,1:T(8,128)S(1)}, f32[13,192]{1,0:T(8,128)S(1)}) all-reduce(bf16[192,2304]{1,0:T(8,128)(2,1)} %reduce-scatter.8.cloned.1.call-done, ...), channel_id=1, replica_groups=mesh['dp'=8,'fsdp'=4] {'dp'}, use_global_device_ids=true, to_apply=%region_17.18 | all-reduce | flops 1771968 | bytes 10631808 | tf_op jit(solution)/shard_map/psum | solution.py:293
  743.1 6.6 multiply_reduce_fusion.13
  749.8 5.8 multiply_reduce_fusion.9
  755.6 5.4 multiply_reduce_fusion.10
  761.0 3.2 pad_maximum_fusion.4
  764.2 3.2 pad_maximum_fusion.3
  767.4 2.9 convert_element_type.154
  770.2 6.5 all-reduce.2
  781.2 3.5 multiply_subtract_fusion
  (205 shorter events, 40.7 us)
Async XLA Ops:
  7.2 36.5 %all-gather.6.cloned.1.call-start = ((), (), s32[]{:S(2)}) async-start(), calls=%async_computation.5 | async-start | bytes 4423680 | tf_op jit(solution)/shard_map/all_gather | solution.py:258
  9.8 117.3 %all-gather.8.cloned.1.call-start = ((), (), s32[]{:S(2)}) async-start(), calls=%async_computation.6 | async-start | bytes 1474560 | tf_op jit(solution)/shard_map/all_gather | solution.py:259
  10.6 122.9 %all-gather.10.cloned.1.call-start = ((), (), s32[]{:S(2)}) async-start(), calls=%async_computation.7 | async-start | bytes 5898240 | tf_op jit(solution)/shard_map/all_gather | solution.py:260
  13.5 8.5 %copy-start.53 = (s32[5,40]{1,0:T(8,128)S(1)}, s32[5,40]{1,0:T(8,128)}, u32[]{:S(2)}) copy-start(s32[5,40]{1,0:T(8,128)} %param.22) | copy-start | bytes 2404
  13.5 8.5 %copy-start.54 = (s32[5]{0:T(128)S(1)}, s32[5]{0:T(128)}, u32[]{:S(2)}) copy-start(s32[5]{0:T(128)} %param.21) | copy-start | bytes 64
  13.6 154.1 %all-gather.12.cloned.1.call-start = ((), (), s32[]{:S(2)}) async-start(), calls=%async_computation.8 | async-start | bytes 5898240 | tf_op jit(solution)/shard_map/all_gather | solution.py:261
  14.8 9.9 %copy-start.9 = (bf16[5,185,768]{2,1,0:T(8,128)(2,1)S(1)}, bf16[5,185,768]{2,1,0:T(8,128)(2,1)}, u32[]{:S(2)}) copy-start(bf16[5,185,768]{2,1,0:T(8,128)(2,1)} %param.19) | copy-start | bytes 4262404
  14.8 10.8 %copy-start.22 = (bf16[5,185,768]{2,1,0:T(8,128)(2,1)S(1)}, bf16[5,185,768]{2,1,0:T(8,128)(2,1)}, u32[]{:S(2)}) copy-start(bf16[5,185,768]{2,1,0:T(8,128)(2,1)} %param.20) | copy-start | bytes 4262404
  14.8 304.5 %reduce-scatter.16.cloned.1.call-start = ((), (), s32[]{:S(2)}) async-start(), calls=%async_computation.13 | async-start | bytes 245760
  22.0 21.7 %copy-start.42 = (f32[768]{0:T(1024)}, f32[768]{0:T(1024)S(1)}, u32[]{:S(2)}) copy-start(f32[768]{0:T(1024)S(1)} %get-tuple-element.33) | copy-start | bytes 9220
  22.1 6.4 copy-start.38
  24.7 18.9 %copy-start.44 = (f32[925]{0:T(1024)}, f32[925]{0:T(1024)S(1)}, u32[]{:S(2)}) copy-start(f32[925]{0:T(1024)S(1)} %div.118) | copy-start | bytes 11104
  28.5 15.2 %copy-start.46 = (f32[925]{0:T(1024)}, f32[925]{0:T(1024)S(1)}, u32[]{:S(2)}) copy-start(f32[925]{0:T(1024)S(1)} %rsqrt.26) | copy-start | bytes 11104
  33.3 17.7 %copy-start.16 = (f32[925,768]{1,0:T(8,128)}, f32[925,768]{1,0:T(8,128)S(1)}, u32[]{:S(2)}) copy-start(f32[925,768]{1,0:T(8,128)S(1)} %reshape.206) | copy-start | bytes 8524804
  90.8 8.3 %copy-start.4 = (bf16[5,185,1,12,64]{1,4,3,0,2:T(8,128)(2,1)}, bf16[5,185,1,12,64]{1,4,3,0,2:T(8,128)(2,1)S(1)}, u32[]{:S(2)}) copy-start(bf16[5,185,1,12,64]{1,4,3,0,2:T(8,128)(2,1)S(1)} %copy.86) | copy-start | bytes 4262404
  99.1 17.5 %copy-start.32 = (bf16[5,185,1,12,64]{1,4,3,0,2:T(8,128)(2,1)S(1)}, bf16[5,185,1,12,64]{1,4,3,0,2:T(8,128)(2,1)}, u32[]{:S(2)}) copy-start(bf16[5,185,1,12,64]{1,4,3,0,2:T(8,128)(2,1)} %copy.84) | copy-start | bytes 4262404
  133.5 34.1 %copy-start.10 = (f32[925,768]{1,0:T(8,128)S(1)}, f32[925,768]{1,0:T(8,128)}, u32[]{:S(2)}) copy-start(f32[925,768]{1,0:T(8,128)} %reshape.209) | copy-start | bytes 8524804
  167.7 11.3 %copy-start.13 = (f32[925,768]{1,0:T(8,128)S(1)}, f32[925,768]{1,0:T(8,128)}, u32[]{:S(2)}) copy-start(f32[925,768]{1,0:T(8,128)} %copy-done.12) | copy-start | bytes 8524804
  167.7 11.3 %copy-start.55 = (bf16[768,3072]{1,0:T(8,128)(2,1)S(1)}, bf16[768,3072]{1,0:T(8,128)(2,1)}, u32[]{:S(2)}) copy-start(bf16[768,3072]{1,0:T(8,128)(2,1)} %all-gather.10.cloned.1.call-done) | copy-start | bytes 14155780
  178.9 5.2 copy-start.57
  192.4 14.4 %slice-start = ((s8[11796480]{0:T(1024)(128)(4,1)}), s8[3407872]{0:T(1024)(128)(4,1)S(1)}, s32[]{:S(2)}) async-start(s8[11796480]{0:T(1024)(128)(4,1)} %bitcast.87), calls=%async_computation.14 | async-start | bytes 6815744
  198.4 8.4 %slice-start.1 = ((s8[11796480]{0:T(1024)(128)(4,1)}), s8[4194304]{0:T(1024)(128)(4,1)S(1)}, s32[]{:S(2)}) async-start(s8[11796480]{0:T(1024)(128)(4,1)} %bitcast.87), calls=%async_computation.15 | async-start | bytes 8388608
  198.4 8.4 %slice-start.2 = ((s8[11796480]{0:T(1024)(128)(4,1)}), s8[4194304]{0:T(1024)(128)(4,1)S(1)}, s32[]{:S(2)}) async-start(s8[11796480]{0:T(1024)(128)(4,1)} %bitcast.87), calls=%async_computation.16 | async-start | bytes 8388608
  198.4 8.4 %copy-start.33 = (bf16[5,185,1,12,64]{1,4,3,0,2:T(8,128)(2,1)S(1)}, bf16[5,185,1,12,64]{1,4,3,0,2:T(8,128)(2,1)}, u32[]{:S(2)}) copy-start(bf16[5,185,1,12,64]{1,4,3,0,2:T(8,128)(2,1)} %copy.84) | copy-start | bytes 4262404
  198.4 9.2 %copy-start.34 = (bf16[5,185,12,64]{1,3,2,0:T(8,128)(2,1)S(1)}, bf16[5,185,12,64]{1,3,2,0:T(8,128)(2,1)}, u32[]{:S(2)}) copy-start(bf16[5,185,12,64]{1,3,2,0:T(8,128)(2,1)} %copy.68) | copy-start | bytes 4262404
  213.3 6.7 copy-start.6
  241.8 14.1 %copy-start.17 = (f32[925,768]{1,0:T(8,128)S(1)}, f32[925,768]{1,0:T(8,128)}, u32[]{:S(2)}) copy-start(f32[925,768]{1,0:T(8,128)} %copy-done.16) | copy-start | bytes 8524804
  241.8 14.1 %copy-start.43 = (f32[768]{0:T(1024)S(1)}, f32[768]{0:T(1024)}, u32[]{:S(2)}) copy-start(f32[768]{0:T(1024)} %copy-done.42) | copy-start | bytes 9220
  241.8 14.1 %copy-start.45 = (f32[925]{0:T(1024)S(1)}, f32[925]{0:T(1024)}, u32[]{:S(2)}) copy-start(f32[925]{0:T(1024)} %copy-done.44) | copy-start | bytes 11104
  241.9 14.1 %copy-start.47 = (f32[925]{0:T(1024)S(1)}, f32[925]{0:T(1024)}, u32[]{:S(2)}) copy-start(f32[925]{0:T(1024)} %copy-done.46) | copy-start | bytes 11104
  256.0 8.7 %copy-start.19 = (f32[925,768]{1,0:T(8,128)S(1)}, f32[925,768]{1,0:T(8,128)}, u32[]{:S(2)}) copy-start(f32[925,768]{1,0:T(8,128)} %copy-done.18) | copy-start | bytes 8524804
  256.0 8.7 %copy-start.51 = (pred[925]{0:T(1024)(128)(4,1)S(1)}, pred[925]{0:T(1024)(128)(4,1)}, u32[]{:S(2)}) copy-start(pred[925]{0:T(1024)(128)(4,1)} %broadcast_in_dim.105) | copy-start | bytes 2779
  268.0 5.0 copy-start.23
  268.0 52.3 %reduce-scatter.10.cloned.1.call-start = ((), (), s32[]{:S(2)}) async-start(), calls=%async_computation.10 | async-start | bytes 1474560 | tf_op jit(solution)/shard_map/reduce_scatter | solution.py:280
  272.9 87.5 %reduce-scatter.8.cloned.1.call-start = ((), (), s32[]{:S(2)}) async-start(), calls=%async_computation.9 | async-start | bytes 4423680 | tf_op jit(solution)/shard_map/reduce_scatter | solution.py:277
  281.3 129.5 %reduce-scatter.14.cloned.1.call-start = ((), (), s32[]{:S(2)}) async-start(), calls=%async_computation.12 | async-start | bytes 5898240 | tf_op jit(solution)/shard_map/reduce_scatter | solution.py:286
  292.7 168.7 %reduce-scatter.12.cloned.1.call-start = ((), (), s32[]{:S(2)}) async-start(), calls=%async_computation.11 | async-start | bytes 5898240 | tf_op jit(solution)/shard_map/reduce_scatter | solution.py:283
  319.3 421.4 %copy-start.25 = (f32[768,192]{0,1:T(8,128)S(1)}, f32[768,192]{0,1:T(8,128)}, u32[]{:S(2)}) copy-start(f32[768,192]{0,1:T(8,128)} %param.24) | copy-start | bytes 1769476
  319.3 421.4 %copy-start.36 = (f32[768,192]{0,1:T(8,128)S(1)}, f32[768,192]{0,1:T(8,128)}, u32[]{:S(2)}) copy-start(f32[768,192]{0,1:T(8,128)} %param.30) | copy-start | bytes 1769476
  319.3 421.4 %copy-start.37 = (f32[768,192]{0,1:T(8,128)S(1)}, f32[768,192]{0,1:T(8,128)}, u32[]{:S(2)}) copy-start(f32[768,192]{0,1:T(8,128)} %param.31) | copy-start | bytes 1769476
  743.1 6.7 copy-start.1
  743.1 6.7 copy-start.26
  743.1 6.7 copy-start.27
  743.1 6.7 copy-start.31
  749.8 5.8 copy-start.2
  749.8 5.8 copy-start.28
  749.8 5.8 copy-start.29
  749.8 5.8 copy-start.30
  (22 other events, 52.6 us)
Sparse Core Ops, SparseCore 0:
  10.2 33.4 all-gather.5
  45.8 17.4 all-gather.7
  65.4 37.4 all-gather.9
  104.9 37.4 all-gather.11
  268.1 20.2 reduce-scatter.15
  291.4 25.7 reduce-scatter.9
  319.9 40.4 reduce-scatter.7
  362.9 47.8 reduce-scatter.13
  413.5 47.8 reduce-scatter.11
where the time goes:
time: 805 us; the launch traced here: 797 us
  blocking collectives  292 us (36%)
  waiting for transfers between devices  152 us (19%)
  matrix products  146 us (18%)
  local copies, waits for them, and re-layouts  104 us (13%)
  other arithmetic  84.4 us (10%)
  between operations  17.6 us (2%)
    psum x1, blocking collectives, local(): lax.psum((summed[0], summed[1], summed[2], summed[3], summed[4]), 'dp')  279 us
    reduce_scatter x1, waiting for transfers between devices, local(): lax.psum_scatter(grads[2].astype(jnp.bfloat16), 'fsdp', scatter_dimension...  50.6 us
    reduce_scatter x1, waiting for transfers between devices, local(): lax.psum_scatter(grads[3].astype(jnp.bfloat16), 'fsdp', scatter_dimension...  50.4 us
    reduce_scatter x1, waiting for transfers between devices, local(): lax.psum_scatter(grads[0].astype(jnp.bfloat16), 'fsdp', scatter_dimension...  40.1 us
    dot_general x1, matrix products, run_forward(): jnp.dot(normed_two_low, up_weight, preferred_element_type=jnp.float32)  34.1 us
    unnamed x127, local copies, waits for them, and re-layouts  28.6 us
    reduce_sum x4, other arithmetic, local(): update_squares = jnp.stack([jnp.sum(update * update) for update in updates])  19.9 us
    sub x1, other arithmetic, run_forward(): shifted = scores - jnp.max(scores, axis=-1, keepdims=True)  17.5 us
  transfers between devices with their start and end apart: 9, of which 4 were waited for; matrix products, arithmetic and copies ran while one was open for 23% of the time, Pallas kernels for 0%

commit v1 on v0

v1 whole, which is shorter than its diff:
```python
import functools

import jax
import jax.numpy as jnp
from jax import lax
from jax.experimental import pallas as pl
from jax.experimental.pallas import tpu as pltpu
from jax.sharding import PartitionSpec as P

HEAD = 64
TXT = 40
PATCH = 145
STEP = 7
SEQ = TXT + PATCH
PAD = 192
GROUP = 4
PARTS = 2
TILE = 256

ln_eps = 1e-06
beta_one = 0.5
beta_two = 0.55
adam_eps = 1e-06
decay_rate = 0.01
matrix_rate = 0.5
vector_rate = 0.3

f32 = jnp.float32
bf16 = jnp.bfloat16
ORDER = (0, 2, 1, 3)
NT = (((1,), (1,)), ((), ()))
TN = (((0,), (0,)), ((), ()))

VM = pl.BlockSpec(memory_space=pltpu.VMEM)
SM = pl.BlockSpec(memory_space=pltpu.SMEM)


def dot(left, right, dims=None):
    if dims is None:
        return jnp.dot(left, right, preferred_element_type=f32)
    return lax.dot_general(left, right, dims, preferred_element_type=f32)


def call(body, grid, ins, outs, scratch, limit, args, name, after=(), aliases=None, flops=10**12):
    count = len(ins)

    def run(*refs):
        body(*refs[:count], *refs[count + len(after) :])

    return pl.pallas_call(
        run,
        grid=grid or (),
        in_specs=list(ins) + [pl.BlockSpec(memory_space=pl.ANY)] * len(after),
        out_specs=[o[1] for o in outs],
        out_shape=[o[0] for o in outs],
        input_output_aliases=aliases or {},
        scratch_shapes=scratch,
        compiler_params=pltpu.CompilerParams(vmem_limit_bytes=limit << 20),
        cost_estimate=pl.CostEstimate(flops=flops, bytes_accessed=flops // 100, transcendentals=0),
        name=name,
    )(*args, *after)


def far_mem(shape, dtype):
    return pltpu.HBM(tuple(shape), dtype)


def tie(value, *deps):
    return pl.pallas_call(
        lambda *refs: None,
        in_specs=[pl.BlockSpec(memory_space=pl.ANY)] * (1 + len(deps)),
        out_specs=pl.BlockSpec(memory_space=pl.ANY),
        out_shape=jax.ShapeDtypeStruct(value.shape, value.dtype),
        input_output_aliases={0: 0},
        name="tie",
    )(value, *deps)


def whole(shape):
    return pl.BlockSpec(shape, lambda i: (0,) * len(shape), pipeline_mode=pl.Buffered(1))


def shard_specs(shards, wide, columns):
    specs = [pl.BlockSpec((v.shape[0], wide), lambda i, at=at: (0, at + columns(i))) for v, at in shards]
    return specs, [v for v, _ in shards]


def unit_rows(rows):
    centred = rows - jnp.mean(rows, axis=-1, keepdims=True)
    factor = lax.rsqrt(jnp.mean(centred * centred, axis=-1, keepdims=True) + ln_eps)
    return centred * factor, factor


def unit_back(grad_normed, unit, factor, gain):
    grad_unit = grad_normed * gain
    return factor * (
        grad_unit
        - jnp.mean(grad_unit, axis=-1, keepdims=True)
        - unit * jnp.mean(grad_unit * unit, axis=-1, keepdims=True)
    )


def put_turned(who_ref, value, scratch, out_ref):
    rows = out_ref.shape[0] // 4
    scratch[...] = value.T
    for place, other in enumerate(ORDER):
        start = pl.multiple_of((who_ref[0] ^ other) * rows, 64)
        out_ref[place * rows : (place + 1) * rows, :] = scratch[pl.ds(start, rows), :]


def gather_rows(who_ref, refs, out_ref):
    rows = refs[0].shape[0]
    half = rows // 2
    places = [(0, None), (1, None)]
    places += [(2, None), (3, None)] if len(refs) == 4 else [(2, 0), (2, 1), (3, 0), (3, 1)]
    for (other, part), ref in zip(places, refs):
        start = (who_ref[0] ^ other) * rows
        if part is not None:
            start += (who_ref[1] ^ part) * half
        out_ref[pl.ds(pl.multiple_of(start, 32), ref.shape[0]), :] = ref[...]


def cast_heads_body(w_ref, *outs):
    wide = GROUP * HEAD
    width = w_ref.shape[1] // 3
    for group, out in enumerate(outs):
        for kind in range(3):
            at = kind * width + group * wide
            out[:, kind * wide : (kind + 1) * wide] = w_ref[:, at : at + wide].astype(bf16)


def cast_heads(weight):
    rows, cols = weight.shape
    groups = cols // (3 * GROUP * HEAD)
    out = jax.ShapeDtypeStruct((rows, cols // groups), bf16)
    return call(cast_heads_body, None, [VM], [(out, VM)] * groups, [], 8, (weight,), "cast_heads")


def cast_rest_body(who, out_ref, up_ref, down_ref, o_ref, up_half, down_half, *parts):
    o_ref[...] = out_ref[...].astype(bf16)
    cols = parts[0].shape[1] // 2
    for part, ref in enumerate(parts):
        ref[:, :cols] = up_ref[:, part * cols : (part + 1) * cols].astype(bf16)
        ref[:, cols:] = down_ref[:, part * cols : (part + 1) * cols].astype(bf16)
    half = up_half.shape[0]
    rows = pl.ds(pl.multiple_of(who[1] * half, 32), half)
    up_half[...] = up_ref[rows, :cols].astype(bf16)
    down_half[...] = down_ref[rows, :cols].astype(bf16)


def cast_rest(who, out_t, up, down_t, after):
    rows, hidden = up.shape
    cols = hidden // PARTS
    shapes = [(rows, out_t.shape[1]), (rows // 2, cols), (rows // 2, cols)] + [(rows, 2 * cols)] * PARTS
    outs = [(jax.ShapeDtypeStruct(shape, bf16), VM) for shape in shapes]
    return call(cast_rest_body, None, [SM, VM, VM, VM], outs, [], 8, (who, out_t, up, down_t), "cast_rest", after)


def chosen_rows(mark_ref, length, item):
    marks = mark_ref[:, item : item + 1]
    places = lax.broadcasted_iota(jnp.int32, marks.shape, 0)
    return jnp.where((marks == 1) & (places >= 1) & (places < length), 1.0, 0.0)


def spread_rows(chosen, width):
    return jnp.broadcast_to(chosen, (chosen.shape[0], width)) > 0


def prep_body(who, len_ref, x_ref, g_ref, mark_ref, v0, v1, v2, v3, vec_ref, xb_ref, a_ref, at_ref, dm_ref, dmt_ref, bd_ref, scratch, scratch_two):
    items, _, width = x_ref.shape
    rows, cols = v0.shape
    vec_ref[...] = jnp.zeros_like(vec_ref)
    for block in range(4):
        value = v0[...].astype(f32)
        for other, ref in ((1, v1), (2, v2), (3, v3)):
            value = jnp.where((who[0] ^ other) == block, ref[...].astype(f32), value)
        vec_ref[:rows, block * cols : (block + 1) * cols] = value
    gain, shift, embed = vec_ref[0:1, :], vec_ref[1:2, :], vec_ref[12:13, :]
    tail = jnp.zeros((PAD - SEQ, width), f32)
    for item in range(items):
        rows = slice(item * PAD, (item + 1) * PAD)
        x = x_ref[item].astype(f32)
        marked = spread_rows(chosen_rows(mark_ref, len_ref[item], item), width)
        x = jnp.concatenate([jnp.where(marked, embed, x[:TXT]), x[TXT:], tail], axis=0)
        xb_ref[rows, :] = x.astype(bf16)
        unit, _ = unit_rows(x)
        a_ref[rows, :] = (unit * gain + shift).astype(bf16)
        dm_ref[rows, :] = jnp.concatenate([g_ref[item].astype(f32), tail], axis=0).astype(bf16)
    bd_ref[...] = jnp.sum(dm_ref[...].astype(f32), axis=0, keepdims=True)
    put_turned(who, a_ref[...], scratch, at_ref)
    put_turned(who, dm_ref[...], scratch_two, dmt_ref)


def prep(who, lengths, block_in, out_grad, marks_t, vec_shards):
    items, _, width = block_in.shape
    rows = items * PAD
    near = jax.ShapeDtypeStruct((rows, width), bf16)
    flat, turned = far_mem((rows, width), bf16), far_mem((width, rows), bf16)
    return call(
        prep_body,
        None,
        [SM, SM, VM, VM, VM, VM, VM, VM, VM],
        [
            (jax.ShapeDtypeStruct((16, width), f32), VM),
            (flat, VM),
            (near, VM),
            (turned, VM),
            (flat, VM),
            (turned, VM),
            (jax.ShapeDtypeStruct((1, width), f32), VM),
        ],
        [pltpu.VMEM((width, rows), bf16)] * 2,
        20,
        (who, lengths, block_in, out_grad, marks_t, *vec_shards),
        "prep",
    )


def key_mask(length):
    places = lax.broadcasted_iota(jnp.int32, (PAD, 1), 0)
    return ((places >= TXT) & (places < SEQ)) | (places < length)


def half_masks():
    lanes = lax.broadcasted_iota(jnp.int32, (1, 2 * HEAD), 1)
    low = jnp.where(lanes < HEAD, 1.0, 0.0)
    return low.astype(bf16), (1.0 - low).astype(bf16)


def attend_body(group, who, len_ref, a_ref, vec_ref, *rest):
    wide = GROUP * HEAD
    shards, (qkv_ref, o_ref, st_ref, w_ref) = rest[:-4], rest[-4:]
    gather_rows(who, shards, w_ref)
    cols = slice(group * wide, (group + 1) * wide)
    bias = jnp.concatenate([vec_ref[2:3, cols], jnp.zeros((1, wide), f32), vec_ref[3:4, cols]], axis=1)
    qkv_ref[...] = (dot(a_ref[...], w_ref[...]) + bias).astype(bf16)
    halves = half_masks()

    @pl.loop(0, len_ref.shape[0])
    def _(item):
        rows = pl.ds(pl.multiple_of(item * PAD, PAD), PAD)
        valid = key_mask(len_ref[item])
        for pair in range(GROUP // 2):
            at = pair * 2 * HEAD
            q = qkv_ref[rows, at : at + 2 * HEAD]
            k = qkv_ref[rows, wide + at : wide + at + 2 * HEAD]
            v = qkv_ref[rows, 2 * wide + at : 2 * wide + at + 2 * HEAD]
            out = None
            for half in range(2):
                s = dot(k * halves[half], q, NT) * HEAD ** (-0.5)
                s = jnp.where(valid, s, -1000000000.0)
                top = jnp.max(s, axis=0, keepdims=True)
                e = jnp.exp(s - top)
                scale = 1.0 / jnp.sum(e, axis=0, keepdims=True)
                p = (e * scale).astype(bf16)
                part = dot(p, v * halves[half], TN)
                out = part if out is None else out + part
                head = 2 * pair + half
                st_ref[item, head : head + 1, :] = top
                st_ref[item, GROUP + head : GROUP + head + 1, :] = scale
            o_ref[rows, at : at + 2 * HEAD] = out.astype(bf16)


def attend(who, lengths, a, weights, vecs, group, after):
    rows, width = a.shape
    wide = GROUP * HEAD
    items = lengths.shape[0]
    specs, arrays = shard_specs(weights, 3 * wide, lambda i: 0)
    return call(
        functools.partial(attend_body, group),
        (1,),
        [SM, SM, whole(a.shape), whole(vecs.shape)] + specs,
        [
            (far_mem((rows, 3 * wide), bf16), whole((rows, 3 * wide))),
            (jax.ShapeDtypeStruct((rows, wide), bf16), whole((rows, wide))),
            (far_mem((items, 2 * GROUP, PAD), f32), whole((items, 2 * GROUP, PAD))),
        ],
        [pltpu.VMEM((width, 3 * wide), bf16)],
        16,
        (who, lengths, a, vecs, *arrays),
        "attend",
        after,
    )


def mix_body(who, x_ref, o0, o1, o2, vec_ref, *rest):
    shards, (y_ref, c_ref, ct_ref, w_ref, scratch) = rest[:-5], rest[-5:]
    gather_rows(who, shards, w_ref)
    wide = GROUP * HEAD
    acc = x_ref[...].astype(f32) + vec_ref[4:5, :]
    for group, o in enumerate((o0, o1, o2)):
        acc += dot(o[...], w_ref[:, group * wide : (group + 1) * wide], NT)
    y_ref[...] = acc
    unit, _ = unit_rows(acc)
    c_ref[...] = (unit * vec_ref[5:6, :] + vec_ref[6:7, :]).astype(bf16)
    put_turned(who, c_ref[...], scratch, ct_ref)


def mix(who, xb, outs, weights, vecs, after):
    rows, width = xb.shape
    specs, arrays = shard_specs(weights, width, lambda i: 0)
    return call(
        mix_body,
        (1,),
        [SM, whole(xb.shape)] + [whole(o.shape) for o in outs] + [whole(vecs.shape)] + specs,
        [
            (far_mem((rows, width), f32), whole((rows, width))),
            (jax.ShapeDtypeStruct((rows, width), bf16), whole((rows, width))),
            (jax.ShapeDtypeStruct((width, rows), bf16), whole((width, rows))),
        ],
        [pltpu.VMEM((width, width), bf16), pltpu.VMEM((width, rows), bf16)],
        18,
        (who, xb, *outs, vecs, *arrays),
        "mix",
        after,
    )


def gelu_pair(h):
    bell = jnp.exp(-0.5 * h * h)
    t = 1.0 / (1.0 + (0.3275911 * 0.7071067811865476) * jnp.abs(h))
    poly = t * (0.127414796 + t * (-0.142248368 + t * (0.7107068705 + t * (-0.7265760135 + t * 0.5307027145))))
    tail = poly * bell
    return jnp.where(h < 0, tail, 1.0 - tail), bell


def ffn_body(first, counts, base, who, c_ref, dm_ref, ct_ref, dmt_ref, *rest):
    ups, downs, rest = rest[: counts[0]], rest[counts[0] : sum(counts)], rest[sum(counts) :]
    if first:
        bu_ref, gk_ref, gs_ref, gelu_ref, gbu_ref, dc_ref, up_w, down_w = rest
    else:
        bu_ref, dc_in, gk_ref, gs_ref, gelu_ref, gbu_ref, dc_ref, up_w, down_w = rest

    @pl.when(pl.program_id(0) == 0)
    def _():
        dc_ref[...] = jnp.zeros_like(dc_ref) if first else dc_in[...]

    gather_rows(who, ups, up_w)
    gather_rows(who, downs, down_w)
    row = (base + pl.program_id(0)) // (c_ref.shape[1] // TILE)
    h = dot(c_ref[...], up_w[...]) + bu_ref[pl.ds(row, 1), :]
    phi, bell = gelu_pair(h)
    gelu = (h * phi).astype(bf16)
    gelu_ref[...] = gelu
    slope = phi + h * bell * 0.3989422804014327
    dh = (dot(dm_ref[...], down_w[...]) * slope).astype(bf16)
    gbu_ref[...] = jnp.sum(dh.astype(f32), axis=0, keepdims=True)
    half = gk_ref.shape[1]
    grad = dot(ct_ref[...], dh).astype(bf16)
    gk_ref[0], gs_ref[0] = grad[:half], grad[half:]
    grad = dot(dmt_ref[...], gelu).astype(bf16)
    gk_ref[1], gs_ref[1] = grad[:half], grad[half:]
    dc_ref[...] += dot(dh, up_w[...], NT)


def ffn(who, c, dm, ct, dmt, ups, downs, vecs, dc, part, after):
    rows, width = c.shape
    cols = 4 * width // PARTS
    base, across = part * cols // TILE, width // TILE
    up_specs, up_arrays = shard_specs(ups, TILE, lambda i: i)
    down_specs, down_arrays = shard_specs(downs, TILE, lambda i: i)
    half = jax.ShapeDtypeStruct((2, width // 2, cols), bf16)
    hspec = pl.BlockSpec((2, width // 2, TILE), lambda i: (0, 0, i))
    return call(
        functools.partial(ffn_body, dc is None, (len(ups), len(downs)), base),
        (cols // TILE,),
        [SM, whole(c.shape), whole(dm.shape), whole(ct.shape), whole(dmt.shape)]
        + up_specs
        + down_specs
        + [pl.BlockSpec((8, TILE), lambda i: (1, (base + i) % across))]
        + ([] if dc is None else [whole(dc.shape)]),
        [
            (half, hspec),
            (half, hspec),
            (far_mem((rows, cols), bf16), pl.BlockSpec((rows, TILE), lambda i: (0, i))),
            (jax.ShapeDtypeStruct((1, cols), f32), pl.BlockSpec((1, TILE), lambda i: (0, i))),
            (jax.ShapeDtypeStruct((rows, width), f32), whole((rows, width))),
        ],
        [pltpu.VMEM((width, TILE), bf16), pltpu.VMEM((width, TILE), bf16)],
        30,
        (who, c, dm, ct, dmt, *up_arrays, *down_arrays, vecs) + (() if dc is None else (dc,)),
        "ffn",
        after,
    )


def turn_body(who, dc_ref, y_ref, dm_ref, o0, o1, o2, vec_ref, *rest):
    shards, rest = rest[:-10], rest[-10:]
    dy_ref, gk_ref, gs_ref, do0, do1, do2, gv_ref, w_ref, scratch, drt_ref = rest
    gather_rows(who, shards, w_ref)
    wide = GROUP * HEAD
    dc = dc_ref[...]
    unit, factor = unit_rows(y_ref[...])
    gv_ref[0:1, :] = jnp.sum(dc * unit, axis=0, keepdims=True)
    gv_ref[1:2, :] = jnp.sum(dc, axis=0, keepdims=True)
    dy = dm_ref[...].astype(f32) + unit_back(dc, unit, factor, vec_ref[5:6, :])
    dy_ref[...] = dy
    dr = dy.astype(bf16)
    gv_ref[2:3, :] = jnp.sum(dr.astype(f32), axis=0, keepdims=True)
    put_turned(who, dr, scratch, drt_ref)
    half = gk_ref.shape[0]
    for group, (o, do) in enumerate(((o0, do0), (o1, do1), (o2, do2))):
        cols = slice(group * wide, (group + 1) * wide)
        do[...] = dot(dr, w_ref[:, cols]).astype(bf16)
        grad = dot(drt_ref[...], o[...]).astype(bf16)
        gk_ref[:, cols] = grad[:half]
        gs_ref[:, cols] = grad[half:]


def turn(who, dc, y, dm, outs, weights, vecs, after):
    rows, width = y.shape
    half = jax.ShapeDtypeStruct((width // 2, width), bf16)
    do = jax.ShapeDtypeStruct((rows, GROUP * HEAD), bf16)
    specs, arrays = shard_specs(weights, width, lambda i: 0)
    results = [far_mem((rows, width), f32), half, half, do, do, do, jax.ShapeDtypeStruct((3, width), f32)]
    return call(
        turn_body,
        (1,),
        [SM, whole(dc.shape), whole(y.shape), whole(dm.shape)] + [whole(o.shape) for o in outs] + [whole(vecs.shape)] + specs,
        [(r, whole(r.shape)) for r in results],
        [pltpu.VMEM((width, width), bf16), pltpu.VMEM((width, rows), bf16), pltpu.VMEM((width, rows), bf16)],
        28,
        (who, dc, y, dm, *outs, vecs, *arrays),
        "turn",
        after,
    )


def attend_back_body(len_ref, qkv_ref, do_ref, st_ref, at_ref, d_ref, gk_ref, gs_ref, gb_ref):
    wide = GROUP * HEAD
    halves = half_masks()

    @pl.loop(0, len_ref.shape[0])
    def _(item):
        rows = pl.ds(pl.multiple_of(item * PAD, PAD), PAD)
        valid = key_mask(len_ref[item])
        for pair in range(GROUP // 2):
            at = pair * 2 * HEAD
            q = qkv_ref[rows, at : at + 2 * HEAD]
            k = qkv_ref[rows, wide + at : wide + at + 2 * HEAD]
            v = qkv_ref[rows, 2 * wide + at : 2 * wide + at + 2 * HEAD]
            do = do_ref[rows, at : at + 2 * HEAD]
            dq = dk = dv = jnp.zeros((PAD, 2 * HEAD), f32)
            for half in range(2):
                head = 2 * pair + half
                km = k * halves[half]
                s = dot(km, q, NT) * HEAD ** (-0.5)
                s = jnp.where(valid, s, -1000000000.0)
                p = jnp.exp(s - st_ref[item, head : head + 1, :]) * st_ref[item, GROUP + head : GROUP + head + 1, :]
                dv += dot(p.astype(bf16), do * halves[half])
                dp = dot(v * halves[half], do, NT)
                delta = jnp.sum(dp * p, axis=0, keepdims=True)
                ds = (p * (dp - delta)).astype(bf16)
                dk += dot(ds, q * halves[half])
                dq += dot(ds, km, TN)
            d_ref[rows, at : at + 2 * HEAD] = (dq * HEAD ** (-0.5)).astype(bf16)
            d_ref[rows, wide + at : wide + at + 2 * HEAD] = (dk * HEAD ** (-0.5)).astype(bf16)
            d_ref[rows, 2 * wide + at : 2 * wide + at + 2 * HEAD] = dv.astype(bf16)

    half = gk_ref.shape[0]
    grad = dot(at_ref[...], d_ref[...]).astype(bf16)
    gk_ref[...] = grad[:half]
    gs_ref[...] = grad[half:]
    gb_ref[...] = jnp.sum(d_ref[...].astype(f32), axis=0, keepdims=True)


def attend_back(lengths, qkv, do, stats, at, after):
    rows, wide3 = qkv.shape
    width = at.shape[0]
    half = jax.ShapeDtypeStruct((width // 2, wide3), bf16)
    return call(
        attend_back_body,
        None,
        [SM, VM, VM, VM, VM],
        [
            (jax.ShapeDtypeStruct((rows, wide3), bf16), VM),
            (half, VM),
            (half, VM),
            (jax.ShapeDtypeStruct((1, wide3), f32), VM),
        ],
        [],
        16,
        (lengths, qkv, do, stats, at),
        "attend_back",
        after,
    )


def start_back_body(counts, who, len_ref, d0, d1, d2, xb_ref, dy_ref, mark_ref, vec_ref, gb0, gb1, gb2, mid_ref, bd_ref, bu0, bu1, *rest):
    shards, (out_ref, gv_ref, w_ref, da_ref) = rest[:-4], rest[-4:]
    at = 0
    wide3 = d0.shape[1]
    acc = None
    for group, d in enumerate((d0, d1, d2)):
        gather_rows(who, shards[at : at + counts[group]], w_ref.at[group])
        at += counts[group]
        part = dot(d[...], w_ref[group], NT)
        acc = part if acc is None else acc + part
    da_ref[...] = acc
    gain_grad = shift_grad = embed_grad = jnp.zeros((1, xb_ref.shape[1]), f32)
    for item in range(out_ref.shape[0]):
        rows = slice(item * PAD, (item + 1) * PAD)
        da = da_ref[rows, :]
        unit, factor = unit_rows(xb_ref[rows, :].astype(f32))
        gain_grad += jnp.sum(da * unit, axis=0, keepdims=True)
        shift_grad += jnp.sum(da, axis=0, keepdims=True)
        dx = dy_ref[rows, :] + unit_back(da, unit, factor, vec_ref[0:1, :])
        marked = spread_rows(chosen_rows(mark_ref, len_ref[item], item), dx.shape[1])
        text = dx[:TXT]
        embed_grad += jnp.sum(jnp.where(marked, text, 0.0), axis=0, keepdims=True)
        out_ref[item] = jnp.concatenate([jnp.where(marked, 0.0, text), dx[TXT:SEQ]], axis=0)
    wide, width = GROUP * HEAD, gv_ref.shape[1]
    gv_ref[...] = jnp.zeros_like(gv_ref)
    gv_ref[0:1, :] = gain_grad
    gv_ref[1:2, :] = shift_grad
    for group, gb in enumerate((gb0, gb1, gb2)):
        gv_ref[2:3, group * wide : (group + 1) * wide] = gb[:, :wide]
        gv_ref[3:4, group * wide : (group + 1) * wide] = gb[:, 2 * wide :]
    gv_ref[4:5, :] = mid_ref[2:3, :]
    gv_ref[5:7, :] = mid_ref[0:2, :]
    gv_ref[7:8, :] = bd_ref[...]
    for row, (ref, place) in enumerate(((bu0, 0), (bu0, 1), (bu1, 0), (bu1, 1))):
        gv_ref[8 + row : 9 + row, :] = ref[:, place * width : (place + 1) * width]
    gv_ref[12:13, :] = embed_grad


def start_back(who, lengths, grads, weights, xb, dy, marks_t, vecs, sums, after):
    rows, width = xb.shape
    wide3 = grads[0].shape[1]
    specs, arrays = shard_specs([w for ws in weights for w in ws], wide3, lambda i: 0)
    out = jax.ShapeDtypeStruct((rows // PAD, SEQ, width), f32)
    small = jax.ShapeDtypeStruct((16, width), f32)
    return call(
        functools.partial(start_back_body, [len(ws) for ws in weights]),
        (1,),
        [SM, SM] + [whole(v.shape) for v in (*grads, xb, dy, marks_t, vecs, *sums)] + specs,
        [(out, whole(out.shape)), (small, whole(small.shape))],
        [pltpu.VMEM((len(weights), width, wide3), bf16), pltpu.VMEM((rows, width), f32)],
        28,
        (who, lengths, *grads, xb, dy, marks_t, vecs, *sums, *arrays),
        "start_back",
        after,
    )


def finish_body(who, y_ref, g_ref, *rest):
    weights, (vec_ref, acc_ref, w_ref) = rest[:-3], rest[-3:]

    @pl.when(pl.program_id(0) == 0)
    def _():
        acc_ref[...] = y_ref[...] + vec_ref[7:8, :]

    gather_rows(who, weights, w_ref)
    acc_ref[...] += dot(g_ref[...], w_ref[...], NT)


def finish_last_body(who, y_ref, g_ref, *rest):
    weights, (out_ref, acc_ref, w_ref) = rest[:-3], rest[-3:]

    @pl.when(pl.program_id(0) == 0)
    def _():
        acc_ref[...] = y_ref[...]

    gather_rows(who, weights, w_ref)
    acc_ref[...] += dot(g_ref[...], w_ref[...], NT)

    @pl.when(pl.program_id(0) == pl.num_programs(0) - 1)
    def _():
        for item in range(out_ref.shape[0]):
            out_ref[item] = acc_ref[item * PAD : (item + 1) * PAD, :].astype(bf16)[:SEQ]


def finish(who, y, gelu, downs, vecs, after):
    rows, width = y.shape
    step = 768
    last = vecs is None
    out = jax.ShapeDtypeStruct((rows // PAD, SEQ, width) if last else y.shape, bf16 if last else f32)
    specs, arrays = shard_specs([(v, at * TILE // step) for v, at in downs], step, lambda i: i)
    return call(
        finish_last_body if last else finish_body,
        (gelu.shape[1] // step,),
        [SM, whole(y.shape), pl.BlockSpec((rows, step), lambda i: (0, i))]
        + specs
        + ([] if last else [whole(vecs.shape)]),
        [(out, whole(out.shape))],
        ([pltpu.VMEM((rows, width), f32)] if last else []) + [pltpu.VMEM((width, step), bf16)],
        24,
        (who, y, gelu, *arrays) + (() if last else (vecs,)),
        "finish",
        after,
    )[0]


def swap(value, axis, bit):
    size = lax.axis_size(axis)
    return lax.ppermute(value, axis, [(i, i ^ (1 << bit)) for i in range(size)])


def half_of(value, which, dim):
    size = value.shape[dim] // 2
    return lax.dynamic_slice_in_dim(value, which * size, size, dim)


def plus(*arrays):
    return functools.reduce(lambda a, b: a + b, (v.astype(f32) for v in arrays))


def step_call(body, who, ins, shapes, name, after):
    outs = [(jax.ShapeDtypeStruct(shape, dtype), VM) for shape, dtype in shapes]
    return call(body, None, [SM] + [VM] * len(ins), outs, [], 8, (who, *ins), name, after, flops=10**9)


def far_body(who, *refs):
    out, pairs = refs[-1], refs[:-1]
    at = 0
    for keep, got in zip(pairs[0::2], pairs[1::2]):
        for one in range(keep.shape[0]):
            out[at] = plus(keep[one, 1], got[one, 1]).astype(bf16)
            at += 1


def near_body(who, *refs):
    far, send, mine = refs[-3:]
    half = send.shape[1]
    go = pl.ds(pl.multiple_of((1 - who[1]) * half, 32), half)
    stay = pl.ds(pl.multiple_of(who[1] * half, 32), half)
    at = 0
    for keep, got in zip(refs[:-3:2], refs[1:-3:2]):
        for one in range(keep.shape[0]):
            send[at] = plus(keep[one, 0, go], got[one, 0, go], far[at, go]).astype(bf16)
            mine[at] = plus(keep[one, 0, stay], got[one, 0, stay], far[at, stay])
            at += 1


def mid_body(who, keep, got, send, mine):
    half = send.shape[1]
    go = pl.ds(pl.multiple_of((1 - who[2]) * half, 16), half)
    stay = pl.ds(pl.multiple_of(who[2] * half, 16), half)
    send[...] = plus(keep[:, go], got[:, go]).astype(bf16)
    mine[...] = plus(keep[:, stay], got[:, stay])


def add_body(who, one, two, out):
    out[...] = plus(one[...], two[...]).astype(bf16)


def join_body(who, mine, got, out):
    half = mine.shape[1]
    out[:, pl.ds(pl.multiple_of(who[2] * half, 16), half)] = mine[...]
    out[:, pl.ds(pl.multiple_of((1 - who[2]) * half, 16), half)] = got[...]


class Chunk:
    def __init__(self, who, keeps, sends):
        split = lambda v: v.reshape(-1, 2, v.shape[-2] // 2, v.shape[-1])
        self.who = who
        self.pairs = [w for k, s in zip(keeps, sends) for w in (split(k), swap(split(s), "fsdp", 0))]
        self.count = sum(k.shape[0] for k in self.pairs[::2])
        self.rows, self.cols = self.pairs[0].shape[2:]

    def far(self, *after):
        self.out = step_call(far_body, self.who, self.pairs, [((self.count, self.rows, self.cols), bf16)], "far", after)[0]
        return self.out

    def near(self, *after):
        shape = (self.count, self.rows // 2, self.cols)
        got = swap(self.out, "fsdp", 1)
        self.out, self.mine = step_call(near_body, self.who, [*self.pairs, got], [(shape, bf16), (shape, f32)], "near", after)
        return self.out

    def mid(self, *after):
        shape = (self.count, self.rows // 4, self.cols)
        got = swap(self.out, "dp", 0)
        self.out, self.mine = step_call(mid_body, self.who, [self.mine, got], [(shape, bf16), (shape, f32)], "mid", after)
        return self.out

    def rest(self, *after):
        got = swap(self.out, "dp", 1)
        self.out = step_call(add_body, self.who, [self.mine, got], [(got.shape, bf16)], "rest", after)[0]
        return self.out

    def part(self, *after):
        for bit in range(2, lax.axis_size("dp").bit_length() - 1):
            got = swap(self.out, "dp", bit)
            self.out = step_call(add_body, self.who, [self.out, got], [(got.shape, bf16)], "part", after)[0]
        return self.out

    def half(self, *after):
        got = swap(self.out, "dp", 1)
        shape = (self.count, self.rows // 2, self.cols)
        self.out = step_call(join_body, self.who, [self.out, got], [(shape, bf16)], "join", after)[0]
        return self.out

    def halves(self):
        return self.out, swap(self.out, "dp", 0)


def adam_body(chained, who, mine, got, first, second, weight, *rest):
    first_new, second_new, update, sums = rest[-4:]
    low = who[1] == 0
    a, b = mine[0].astype(f32), got[0].astype(f32)
    grad = jnp.concatenate([jnp.where(low, a, b), jnp.where(low, b, a)], axis=0)
    moved = adam_moments(grad, first[...], second[...])
    master = weight[...]
    first_new[...], second_new[...] = moved[0], moved[1]
    change = moved[2] + decay_rate * master
    update[...] = change

    @pl.when(pl.program_id(0) == 0)
    def _():
        sums[...] = jnp.zeros_like(sums)

    sums[0:1, :] += jnp.sum(master * master, axis=0, keepdims=True)
    sums[1:2, :] += jnp.sum(change * change, axis=0, keepdims=True)


def adam(who, halves, first, second, weight, wide, steps, grad_at, column_at, made, after):
    rows = weight.shape[0]
    grad = pl.BlockSpec((1, rows // 2, wide), lambda i: (grad_at(i)[0], 0, grad_at(i)[1]))
    block = pl.BlockSpec((rows, wide), lambda i: (0, column_at(i)))
    full = jax.ShapeDtypeStruct(weight.shape, f32)
    sums = jax.ShapeDtypeStruct((2, wide), f32)
    made = list(made or [])
    return call(
        functools.partial(adam_body, len(made)),
        (steps,),
        [SM, grad, grad, block, block, block] + [pl.BlockSpec(memory_space=pl.ANY)] * len(made),
        [(full, block), (full, block), (full, block), (sums, whole(sums.shape))],
        [],
        14,
        (who, *halves, first, second, weight, *made),
        "adam",
        after,
        {6 + k: k for k in range(len(made))},
    )


def total_body(*refs):
    *parts, out = refs
    for row, group in enumerate(parts_of(parts)):
        for kind in range(2):
            value = sum(jnp.sum(ref[kind : kind + 1, :]) for ref in group)
            out[4 * kind + row : 4 * kind + row + 1, :] = jnp.full((1, out.shape[1]), value, f32)


def parts_of(parts):
    return parts[0:2], parts[2:3], parts[3:5], parts[5:7]


def totals(sums):
    out = jax.ShapeDtypeStruct((8, 128), f32)
    return call(total_body, None, [VM] * len(sums), [(out, VM)], [], 8, tuple(sums), "totals")[0]


def apply_body(one, two, w0, w1, w2, w3, u0, u1, u2, u3, n0, n1, n2, n3, norms):
    total = one[...] + two[...]
    norms[...] = jnp.sqrt(total)
    for row, (w, u, n) in enumerate(((w0, u0, n0), (w1, u1, n1), (w2, u2, n2), (w3, u3, n3))):
        ratio = jnp.sqrt(total[row : row + 1, :1]) * lax.rsqrt(total[4 + row : 5 + row, :1] + adam_eps)
        n[...] = w[...] - (matrix_rate * ratio) * u[...]


def apply(one, two, weights, updates):
    steps = 3
    blocks = [pl.BlockSpec((w.shape[0], w.shape[1] // steps), lambda i: (0, i)) for w in weights]
    norms = jax.ShapeDtypeStruct(one.shape, f32)
    return call(
        apply_body,
        (steps,),
        [whole(one.shape)] * 2 + blocks + blocks,
        [(jax.ShapeDtypeStruct(w.shape, f32), b) for w, b in zip(weights, blocks)] + [(norms, whole(one.shape))],
        [],
        24,
        (one, two, *weights, *updates),
        "apply",
    )


def vector_body(who, one, two, first, second, params, new, first_new, second_new):
    rows, cols = params.shape
    total = one[...] + two[...]
    grad = total[:rows, :cols]
    for block in range(1, 4):
        grad = jnp.where(who[0] == block, total[:rows, block * cols : (block + 1) * cols], grad)
    moved = adam_moments(grad, first[...], second[...])
    first_new[...], second_new[...] = moved[0], moved[1]
    new[...] = params[...] - vector_rate * moved[2]


def vector_step(who, one, two, first, second, params):
    out = jax.ShapeDtypeStruct(params.shape, f32)
    args = (who, one, two, first, second, params)
    return call(vector_body, None, [SM] + [VM] * 5, [(out, VM)] * 3, [], 8, args, "vector_step")


def adam_moments(grad, first, second):
    first_new = beta_one * first + (1.0 - beta_one) * grad
    second_new = beta_two * second + (1.0 - beta_two) * grad * grad
    direction = (
        first_new
        / (1.0 - beta_one**STEP)
        / (jnp.sqrt(second_new / (1.0 - beta_two**STEP)) + adam_eps)
    )
    return (first_new, second_new, direction)


def local(
    block_in,
    out_grad,
    caption_len,
    mask_marks,
    qkv_weight,
    out_weight,
    up_weight,
    down_weight,
    vector_params,
    qkv_first,
    qkv_second,
    out_first,
    out_second,
    up_first,
    up_second,
    down_first,
    down_second,
    vector_first,
    vector_second,
):
    width = block_in.shape[2]
    hidden = up_weight.shape[1]
    groups = width // (GROUP * HEAD)
    shard = lax.axis_index("fsdp")
    replica = lax.axis_index("dp")
    who = jnp.stack([shard, replica & 1, (replica >> 1) & 1]).astype(jnp.int32)
    cols = hidden // PARTS
    core = lambda v: swap(v, "fsdp", 0)
    far = lambda v: swap(v, "fsdp", 1)
    turned = lambda v: v.T

    own_heads = cast_heads(qkv_weight)
    vec_own = vector_params.astype(bf16)
    far_heads = [far(own_heads[0])]
    vec_far = far(vec_own)
    far_heads += [far(v) for v in own_heads[1:]]
    own_out, half_up, half_down, *own_parts = cast_rest(
        who, out_weight.T, up_weight, down_weight.T, [own_heads[0]]
    )
    far_out, far_up, far_down, far_part = (far(v) for v in (own_out, half_up, half_down, own_parts[1]))
    vec_shards = [vec_own, core(vec_own), vec_far, core(vec_far)]
    core_parts = [core(v) for v in own_parts]
    first_block = lambda *arrays: [(v, 0) for v in arrays]
    heads_full = [first_block(own, core(own), other, core(other)) for own, other in zip(own_heads, far_heads)]
    out_full = first_block(own_out, core(own_out), far_out, core(far_out))

    marks_t = mask_marks.T
    vecs, xb, a, at, dm, dmt, grad_bd = prep(who, caption_len, block_in, out_grad, marks_t, vec_shards)
    heads = []
    for g in range(groups):
        waits = [h[1] for h in heads[-1:]]
        if g == 2:
            mine_up = tie(far_up, *waits)
            waits.append(mine_up)
        heads.append(attend(who, caption_len, a, heads_full[g], vecs, g, waits))
    mine_down = tie(far_down, heads[-1][1])
    outs = [h[1] for h in heads]
    y, c, ct = mix(who, xb, outs, out_full, vecs, [mine_down])
    tile = cols // TILE
    sides = lambda mine: (mine, swap(mine, "dp", 0))
    pair = lambda own, at: [(own, at), (core(own), at)]
    up_far, down_far = sides(mine_up), sides(mine_down)
    part0 = [(own_parts[0], 0), (core_parts[0], 0)]
    part0_down = [(own_parts[0], tile), (core_parts[0], tile)]
    ups = part0 + first_block(*up_far, *(core(v) for v in up_far))
    downs = part0_down + first_block(*down_far, *(core(v) for v in down_far))
    ffn0 = ffn(who, c, dm, ct, dmt, ups, downs, vecs, None, 0, [])
    chunk_a = Chunk(who, [ffn0[0]], [ffn0[1]])
    result = finish(who, y, ffn0[2], downs, vecs, [])
    far_part = tie(far_part, result)
    shards1 = (own_parts[1], core_parts[1], far_part, core(far_part))
    ups1 = [(v, 0) for v in shards1]
    downs1 = [(v, tile) for v in shards1]
    ffn1 = ffn(who, c, dm, ct, dmt, ups1, downs1, vecs, ffn0[4], 1, [chunk_a.far(result)])
    chunk_b = Chunk(who, [ffn1[0]], [ffn1[1]])
    block_out = finish(who, result, ffn1[2], downs1, None, [])
    sent_b = chunk_b.far(block_out)
    sent_a = chunk_a.near(sent_b)
    dy, out_keep, out_send, *dos, grad_mid = turn(who, ffn1[4], y, dm, outs, out_full, vecs, [sent_b, sent_a])
    back0 = attend_back(caption_len, heads[0][0], dos[0], heads[0][2], at, [])
    chunk_c = Chunk(who, [out_keep, back0[1]], [out_send, back0[2]])
    sent_a = chunk_a.mid(back0[0])
    sent_c = chunk_c.far(sent_a)
    back1 = attend_back(caption_len, heads[1][0], dos[1], heads[1][2], at, [sent_a, sent_c])
    sent_a = chunk_a.rest(back1[0])
    back2 = attend_back(caption_len, heads[2][0], dos[2], heads[2][2], at, [sent_a])
    backs = [back0, back1, back2]
    chunk_d = Chunk(who, [back1[1], back2[1]], [back1[2], back2[2]])
    sent_b = chunk_b.near(back2[0])
    sent_a = chunk_a.part(sent_b)
    sent_d = chunk_d.far(sent_a)
    sent_c = chunk_c.near(sent_d)
    sums = [b[3] for b in backs] + [grad_mid, grad_bd, ffn0[3], ffn1[3]]
    input_grad, vector_grads = start_back(
        who,
        caption_len,
        [b[0] for b in backs],
        heads_full,
        xb,
        dy,
        marks_t,
        vecs,
        sums,
        [sent_a, sent_b, sent_c, sent_d],
    )
    sent_a = chunk_a.half(input_grad)
    sent_b = chunk_b.mid(sent_a)
    vector_one = vector_grads + core(vector_grads)
    sent_d = chunk_d.near(sent_b)
    sent_c = chunk_c.mid(sent_d)
    vector_one = vector_one + far(vector_one)

    qkv = (qkv_first, qkv_second, qkv_weight)
    out = tuple(turned(v) for v in (out_first, out_second, out_weight))
    up = (up_first, up_second, up_weight)
    down = tuple(turned(v) for v in (down_first, down_second, down_weight))
    wide = 2 * TILE
    per = cols // wide

    sent_b = chunk_b.rest(sent_c)
    sent_d = chunk_d.mid(sent_b)
    sent_c = chunk_c.rest(sent_d)
    halves_a = chunk_a.halves()
    up_made = adam(who, halves_a, *up, wide, per, lambda i: (0, i), lambda i: i, None, [sent_c])
    sent_b = chunk_b.part(up_made[3])
    sent_d = chunk_d.rest(sent_b)
    sent_c = chunk_c.part(sent_d)
    down_made = adam(who, halves_a, *down, wide, per, lambda i: (1, i), lambda i: i, None, [sent_c])
    sent_b = chunk_b.half(down_made[3])
    sent_d = chunk_d.part(sent_b)
    sent_c = chunk_c.half(sent_d)
    sent_d = chunk_d.half(sent_c)
    for bit in range(lax.axis_size("dp").bit_length() - 1):
        got = swap(vector_one, "dp", bit)
        if bit < lax.axis_size("dp").bit_length() - 2:
            vector_one = vector_one + got
    halves_c = chunk_c.halves()
    out_made = adam(who, halves_c, *out, TILE, width // TILE, lambda i: (0, i), lambda i: i, None, [sent_d])
    qkv_made = adam(who, halves_c, *qkv, TILE, 3, lambda i: (1, i), lambda i: groups * i, None, [out_made[3]])
    halves_b = chunk_b.halves()
    up_last = adam(who, halves_b, *up, wide, per, lambda i: (0, i), lambda i: per + i, up_made[:3], [qkv_made[3]])
    down_last = adam(who, halves_b, *down, wide, per, lambda i: (1, i), lambda i: per + i, down_made[:3], [up_last[3]])
    qkv_last = adam(
        who,
        chunk_d.halves(),
        *qkv,
        TILE,
        3 * (groups - 1),
        lambda i: (i // 3, i % 3),
        lambda i: groups * (i % 3) + 1 + i // 3,
        qkv_made[:3],
        [down_last[3]],
    )
    vector_new, vector_first_new, vector_second_new = vector_step(
        who, vector_one, got, vector_first, vector_second, vector_params
    )
    squares = totals([qkv_made[3], qkv_last[3], out_made[3], up_made[3], up_last[3], down_made[3], down_last[3]])
    squares = squares + core(squares)
    weights = (qkv_weight, out[2], up_weight, down[2])
    made = (qkv_last, out_made, up_last, down_last)
    *new_weights, norms = apply(squares, far(squares), weights, [m[2] for m in made])
    back = (lambda v: v, turned, lambda v: v, turned)
    moments = [f(m[k]) for f, m in zip(back, made) for k in range(2)]
    return (
        block_out,
        input_grad,
        *(f(w) for f, w in zip(back, new_weights)),
        vector_new,
        *moments,
        vector_first_new,
        vector_second_new,
        norms[:, 0].reshape(2, 4),
    )


def solution(mesh):
    placed = (
        P(("dp", "fsdp"), None, None),
        P(("dp", "fsdp"), None, None),
        P(("dp", "fsdp")),
        P(("dp", "fsdp"), None),
        P("fsdp", None),
        P(None, "fsdp"),
        P("fsdp", None),
        P(None, "fsdp"),
        P(None, "fsdp"),
        P("fsdp", None),
        P("fsdp", None),
        P(None, "fsdp"),
        P(None, "fsdp"),
        P("fsdp", None),
        P("fsdp", None),
        P(None, "fsdp"),
        P(None, "fsdp"),
        P(None, "fsdp"),
        P(None, "fsdp"),
    )
    return jax.shard_map(
        local,
        mesh=mesh,
        in_specs=placed,
        out_specs=(
            P(("dp", "fsdp"), None, None),
            P(("dp", "fsdp"), None, None),
            P("fsdp", None),
            P(None, "fsdp"),
            P("fsdp", None),
            P(None, "fsdp"),
            P(None, "fsdp"),
            P("fsdp", None),
            P("fsdp", None),
            P(None, "fsdp"),
            P(None, "fsdp"),
            P("fsdp", None),
            P("fsdp", None),
            P(None, "fsdp"),
            P(None, "fsdp"),
            P(None, "fsdp"),
            P(None, "fsdp"),
            P(),
        ),
        check_vma=False,
    )
```

time: 805 us -> 349 us (0.43)
  blocking collectives: 292 us -> 0 us
  Pallas kernels: 0 us -> 201 us
  matrix products: 146 us -> 0 us
  waiting for transfers between devices: 152 us -> 58.8 us
  other arithmetic: 84.4 us -> 2.63 us
  local copies, waits for them, and re-layouts: 104 us -> 31.1 us
  starting transfers between devices: 0.37 us -> 47.9 us
  between operations: 17.6 us -> 1.97 us
    psum x2 -> x0, blocking collectives: 286 us -> none  [the longest x1 279 us: local(): lax.psum((summed[0], summed[1], summed[2], summed[3], summed[4]), 'dp')]
    pallas_call x0 -> x53, Pallas kernels: none -> 201 us  [the longest x50 201 us: call(): pl.pallas_call(run, grid=grid or (), in_specs=list(ins) + [pl.BlockSpec(m...]
    dot_general x18 -> x0, matrix products: 146 us -> none  [the longest x1 34.1 us: run_forward(): jnp.dot(normed_two_low, up_weight, preferred_element_type=jnp.float32)]
    reduce_scatter x4 -> x0, waiting for transfers between devices: 141 us -> none  [the longest x1 50.6 us: local(): lax.psum_scatter(grads[2].astype(jnp.bfloat16), 'fsdp', scatter_dimension...]
    ppermute x0 -> x64, waiting for transfers between devices: none -> 58.8 us  [swap(): return lax.ppermute(value, axis, [(i, i ^ 1 << bit) for i in range(size)])]
    reshape x9 -> x0, local copies, waits for them, and re-layouts: 48 us -> none  [the longest x1 14 us: run_backward(): jnp.stack([grad_queries, grad_keys, grad_values], axis=2)]
    ppermute x0 -> x64, starting transfers between devices: none -> 47.9 us  [swap(): return lax.ppermute(value, axis, [(i, i ^ 1 << bit) for i in range(size)])]
    reduce_sum x11 -> x0, other arithmetic: 32.7 us -> none  [the longest x4 19.9 us: local(): update_squares = jnp.stack([jnp.sum(update * update) for update in updates])]
  transfers between devices with their start and end apart: 9 -> 64, of which waited for: 4 -> 16; matrix products, arithmetic and copies ran while one was open for 23% -> 0% of each run, Pallas kernels for 0% -> 56%
where the time goes in v1:
time: 349 us; the launch traced here: 343 us
  Pallas kernels  201 us (58%)
  waiting for transfers between devices  58.8 us (17%)
  starting transfers between devices  47.9 us (14%)
  local copies, waits for them, and re-layouts  31.1 us (9%)
    pallas_call x50, Pallas kernels, call(): pl.pallas_call(run, grid=grid or (), in_specs=list(ins) + [pl.BlockSpec(m...  201 us
    ppermute x64, waiting for transfers between devices, swap(): return lax.ppermute(value, axis, [(i, i ^ 1 << bit) for i in range(size)])  58.8 us
    ppermute x64, starting transfers between devices, swap(): return lax.ppermute(value, axis, [(i, i ^ 1 << bit) for i in range(size)])  47.9 us
    unnamed x223, local copies, waits for them, and re-layouts  30.4 us
  transfers between devices with their start and end apart: 64, of which 16 were waited for; matrix products, arithmetic and copies ran while one was open for 0% of the time, Pallas kernels for 56%

profile of v1, /device:TPU:0, one launch (start us, length us, event | category | flops | bytes accessed | tf_op | source)
XLA Modules:
  0.0 343.0 jit_solution(4071736902974387382)
XLA Ops:
  2.0 3.0 collective-permute-start.1
  11.5 2.6 cast_rest.1
  15.0 2.6 collective-permute-done.4.refs_6_.refs_18_
  20.3 5.5 %prep.1 = (f32[16,768]{1,0:T(8,128)S(1)}, bf16[960,768]{1,0:T(8,128)(2,1)}, bf16[960,768]{1,0:T(8,128)(2,1)S(1)}, bf16[768,960]{1,0:T(8,128)(2,1)}, bf16[960,768...) custom-call(s32[3]{0:T(128)S(1)} %pad_add_fusion.refs_0_, s32[5]{0:T(128)S(1)} %copy-done.55, ...), custom_call_target="tpu_custom_call" | custom-call | flops 999999995904 | bytes 10000000000 | tf_op jit(solution)/shard_map/prep/pallas_call | solution.py:50
  26.6 6.9 %attend.3 = (bf16[960,768]{1,0:T(8,128)(2,1)}, bf16[960,256]{1,0:T(8,128)(2,1)S(1)}, f32[5,8,192]{2,1,0:T(8,128)}) custom-call(s32[3]{0:T(128)S(1)} %pad_add_fusion.refs_0_, s32[5]{0:T(128)S(1)} %copy-done.55, bf16[960,768]{1,0:T(8,128)(2,1)S(1)} %get-tuple-element.129.refs_2_, ...), custom_call_target="tpu_custom_call" | custom-call | flops 999999995904 | bytes 10000000000 | tf_op jit(solution)/shard_map/attend/pallas_call | solution.py:50
  34.0 1.9 collective-permute-start.12
  35.9 6.7 %attend.4 = (bf16[960,768]{1,0:T(8,128)(2,1)}, bf16[960,256]{1,0:T(8,128)(2,1)S(1)}, f32[5,8,192]{2,1,0:T(8,128)}) custom-call(s32[3]{0:T(128)S(1)} %pad_add_fusion.refs_0_, s32[5]{0:T(128)S(1)} %copy-done.55, bf16[960,768]{1,0:T(8,128)(2,1)S(1)} %get-tuple-element.129.refs_2_, ...), custom_call_target="tpu_custom_call" | custom-call | flops 999999995904 | bytes 10000000000 | tf_op jit(solution)/shard_map/attend/pallas_call | solution.py:50
  47.7 6.9 %attend.5 = (bf16[960,768]{1,0:T(8,128)(2,1)}, bf16[960,256]{1,0:T(8,128)(2,1)S(1)}, f32[5,8,192]{2,1,0:T(8,128)}) custom-call(s32[3]{0:T(128)S(1)} %pad_add_fusion.refs_0_, s32[5]{0:T(128)S(1)} %copy-done.55, bf16[960,768]{1,0:T(8,128)(2,1)S(1)} %copy-done.99, f32[16,768]{1,0:T(8,128)S(1)} %get-tuple-element.130.refs_3_.refs_5_.refs_17_.refs_9_.refs_13_.refs_7_.refs_8_, ...), custom_call_target="tpu_custom_call" | custom-call | flops 999999995904 | bytes 10000000000 | tf_op jit(solution)/shard_map/attend/pallas_call | solution.py:50
  57.9 7.5 %collective-permute-done.21.refs_14_.refs_6_ = bf16[96,1536]{1,0:T(8,128)(2,1)} collective-permute-done((bf16[96,1536]{1,0:T(8,128)(2,1)}, bf16[96,1536]{1,0:T(8,128)(2,1)}, u32[]{:S(2)}, u32[]{:S(2)}) %collective-permute-start.21) | collective-permute-done | bytes 294944 | tf_op jit(solution)/shard_map/ppermute | solution.py:596
  65.4 5.9 %collective-permute-done.18.refs_8_ = bf16[96,1536]{1,0:T(8,128)(2,1)} collective-permute-done((bf16[96,1536]{1,0:T(8,128)(2,1)}, bf16[96,1536]{1,0:T(8,128)(2,1)}, u32[]{:S(2)}, u32[]{:S(2)}) %collective-permute-start.18) | collective-permute-done | bytes 294944 | tf_op jit(solution)/shard_map/ppermute | solution.py:596
  72.4 5.4 %mix.1 = (f32[960,768]{1,0:T(8,128)}, bf16[960,768]{1,0:T(8,128)(2,1)S(1)}, bf16[768,960]{1,0:T(8,128)(2,1)S(1)}) custom-call(s32[3]{0:T(128)S(1)} %pad_add_fusion.refs_0_, bf16[960,768]{1,0:T(8,128)(2,1)S(1)} %copy-done.93, bf16[960,256]{1,0:T(8,128)(2,1)S(1)} %copy-done.101, bf16[960,256]{1,0:T(8,128)(2,1)S(1)} %copy-done.9, ...), custom_call_target="tpu_custom_call" | custom-call | flops 999999995904 | bytes 10000000000 | tf_op jit(solution)/shard_map/mix/pallas_call | solution.py:50
  78.5 20.9 %ffn.2 = (bf16[2,384,1536]{2,1,0:T(8,128)(2,1)S(1)}, bf16[2,384,1536]{2,1,0:T(8,128)(2,1)}, bf16[960,1536]{1,0:T(8,128)(2,1)}, f32[1,1536]{1,0:T(1,128)S(1)}, f32[960,768]{1,0:T(8,128)S(1)}) custom-call(s32[3]{0:T(128)S(1)} %pad_add_fusion.refs_0_, bf16[960,768]{1,0:T(8,128)(2,1)S(1)} %get-tuple-element.141.refs_1_, bf16[960,768]{1,0:T(8,128)(2,1)S(1)} %copy-done.88, ...), custom_call_target="tpu_custom_call" | custom-call | flops 999999995904 | bytes 10000000000 | tf_op jit(solution)/shard_map/ffn/pallas_call | solution.py:50
  100.1 3.1 copy-done.74
  103.2 4.8 %finish.2.refs_1_.refs_3_ = f32[960,768]{1,0:T(8,128)S(1)} custom-call(s32[3]{0:T(128)S(1)} %pad_add_fusion.refs_0_, f32[960,768]{1,0:T(8,128)S(1)} %copy-done.75, bf16[960,1536]{1,0:T(8,128)(2,1)S(1)} %copy-done.74, bf16[192,3072]{1,0:T(8,128)(2,1)} %get-tuple-element.145.refs_5_.refs_11_.refs_3_, ...), custom_call_target="tpu_custom_call" | custom-call | flops 999999995904 | bytes 10000000000 | tf_op jit(solution)/shard_map/finish/pallas_call | solution.py:50
  113.2 3.1 far.4.refs_15_
  119.2 20.5 %ffn.3 = (bf16[2,384,1536]{2,1,0:T(8,128)(2,1)S(1)}, bf16[2,384,1536]{2,1,0:T(8,128)(2,1)}, bf16[960,1536]{1,0:T(8,128)(2,1)}, f32[1,1536]{1,0:T(1,128)S(1)}, f32[960,768]{1,0:T(8,128)S(1)}) custom-call(s32[3]{0:T(128)S(1)} %pad_add_fusion.refs_0_, bf16[960,768]{1,0:T(8,128)(2,1)S(1)} %copy-done.92, bf16[960,768]{1,0:T(8,128)(2,1)S(1)} %copy-done.89, ...), custom_call_target="tpu_custom_call" | custom-call | flops 999999995904 | bytes 10000000000 | tf_op jit(solution)/shard_map/ffn/pallas_call | solution.py:50
  141.9 6.0 %finish.3.refs_3_ = bf16[5,185,768]{2,1,0:T(8,128)(2,1)} custom-call(s32[3]{0:T(128)S(1)} %pad_add_fusion.refs_0_, f32[960,768]{1,0:T(8,128)S(1)} %copy-done.1, bf16[960,1536]{1,0:T(8,128)(2,1)S(1)} %copy-done.72, bf16[192,3072]{1,0:T(8,128)(2,1)} %get-tuple-element.147.refs_5_.refs_9_.refs_3_, ...), custom_call_target="tpu_custom_call" | custom-call | flops 999999995904 | bytes 10000000000 | tf_op jit(solution)/shard_map/finish/pallas_call | solution.py:50
  149.3 3.1 far.5.refs_4_.refs_12_
  152.4 3.3 near.4
  157.3 8.3 %turn.1 = (f32[960,768]{1,0:T(8,128)}, bf16[384,768]{1,0:T(8,128)(2,1)S(1)}, bf16[384,768]{1,0:T(8,128)(2,1)S(1)}, bf16[960,256]{1,0:T(8,128)(2,1)S(1)}, bf16[96...) custom-call(s32[3]{0:T(128)S(1)} %pad_add_fusion.refs_0_, ...), custom_call_target="tpu_custom_call" | custom-call | flops 999999995904 | bytes 10000000000 | tf_op jit(solution)/shard_map/turn/pallas_call | solution.py:50
  165.6 7.2 %attend_back.3 = (bf16[960,768]{1,0:T(8,128)(2,1)S(1)}, bf16[384,768]{1,0:T(8,128)(2,1)S(1)}, bf16[384,768]{1,0:T(8,128)(2,1)S(1)}, f32[1,768]{1,0:T(1,128)S(1)}) custom-call(s32[5]{0:T(128)S(1)} %copy-done.55, bf16[960,768]{1,0:T(8,128)(2,1)S(1)} %copy-done.97, bf16[960,256]{1,0:T(8,128)(2,1)S(1)} %get-tuple-element.157.refs_2_, ...), custom_call_target="tpu_custom_call" | custom-call | flops 999999995904 | bytes 10000000000 | tf_op jit(solution)/shard_map/attend_back/pallas_call | solution.py:50
  174.6 1.9 mid.4
  179.9 7.9 %attend_back.4 = (bf16[960,768]{1,0:T(8,128)(2,1)S(1)}, bf16[384,768]{1,0:T(8,128)(2,1)S(1)}, bf16[384,768]{1,0:T(8,128)(2,1)}, f32[1,768]{1,0:T(1,128)S(1)}) custom-call(s32[5]{0:T(128)S(1)} %copy-done.55, bf16[960,768]{1,0:T(8,128)(2,1)S(1)} %copy-done.95, bf16[960,256]{1,0:T(8,128)(2,1)S(1)} %get-tuple-element.162.refs_2_, f32[5,8,192]{2,1,0:T(8,128)S(1)} %copy-done.103, ...), custom_call_target="tpu_custom_call" | custom-call | flops 999999995904 | bytes 10000000000 | tf_op jit(solution)/shard_map/attend_back/pallas_call | solution.py:50
  190.0 7.4 %attend_back.5 = (bf16[960,768]{1,0:T(8,128)(2,1)S(1)}, bf16[384,768]{1,0:T(8,128)(2,1)S(1)}, bf16[384,768]{1,0:T(8,128)(2,1)S(1)}, f32[1,768]{1,0:T(1,128)S(1)}) custom-call(s32[5]{0:T(128)S(1)} %copy-done.55, bf16[960,768]{1,0:T(8,128)(2,1)S(1)} %copy-done.96, bf16[960,256]{1,0:T(8,128)(2,1)S(1)} %get-tuple-element.172.refs_2_, ...), custom_call_target="tpu_custom_call" | custom-call | flops 999999995904 | bytes 10000000000 | tf_op jit(solution)/shard_map/attend_back/pallas_call | solution.py:50
  198.4 2.6 collective-permute-start.34
  202.5 3.1 near.5
  206.2 8.4 %collective-permute-done.34.refs_2_ = bf16[2,48,1536]{2,1,0:T(8,128)(2,1)S(1)} collective-permute-done((bf16[2,48,1536]{2,1,0:T(8,128)(2,1)S(1)}, bf16[2,48,1536]{2,1,0:T(8,128)(2,1)S(1)}, u32[]{:S(2)}, u32[]{:S(2)}) %collective-permute-start.34) | collective-permute-done | bytes 294944 | tf_op jit(solution)/shard_map/ppermute | solution.py:596
  216.0 2.3 far.7.refs_6_.refs_31_
  221.5 9.0 %start_back.1 = (f32[5,185,768]{2,1,0:T(8,128)}, f32[16,768]{1,0:T(8,128)S(1)}) custom-call(s32[3]{0:T(128)S(1)} %pad_add_fusion.refs_0_, s32[5]{0:T(128)S(1)} %copy-done.55, bf16[960,768]{1,0:T(8,128)(2,1)S(1)} %copy-done.63, bf16[960,768]{1,0:T(8,128)(2,1)S(1)} %copy-done.65, bf16[960,768]{1,0:T(8,128)(2,1)S(1)} %get-tuple-element.175.refs_4_, ...), custom_call_target="tpu_custom_call" | custom-call | flops 999999995904 | bytes 10000000000 | tf_op jit(solution)/shard_map/start_back/pallas_call | solution.py:50
  236.3 2.1 collective-permute-start.45
  241.6 4.4 %collective-permute-done.45.refs_2_ = bf16[2,48,1536]{2,1,0:T(8,128)(2,1)S(1)} collective-permute-done((bf16[2,48,1536]{2,1,0:T(8,128)(2,1)S(1)}, bf16[2,48,1536]{2,1,0:T(8,128)(2,1)S(1)}, u32[]{:S(2)}, u32[]{:S(2)}) %collective-permute-start.45) | collective-permute-done | bytes 294944 | tf_op jit(solution)/shard_map/ppermute | solution.py:596
  247.4 2.2 collective-permute-start.48
  249.5 5.1 %collective-permute-done.44.refs_2_ = bf16[2,96,768]{2,1,0:T(8,128)(2,1)S(1)} collective-permute-done((bf16[2,96,768]{2,1,0:T(8,128)(2,1)S(1)}, bf16[2,96,768]{2,1,0:T(8,128)(2,1)S(1)}, u32[]{:S(2)}, u32[]{:S(2)}) %collective-permute-start.44) | collective-permute-done | bytes 294944 | tf_op jit(solution)/shard_map/ppermute | solution.py:596
  259.6 3.3 adam.7
  272.4 3.3 adam.8
  275.7 2.2 collective-permute-done.52.refs_2_
  277.9 1.9 join.5.refs_3_.refs_1_
  285.3 3.3 collective-permute-done.60
  289.4 3.3 collective-permute-done.61
  292.8 4.1 %collective-permute-done.62 = f32[16,768]{1,0:T(8,128)S(1)} collective-permute-done((f32[16,768]{1,0:T(8,128)S(1)}, f32[16,768]{1,0:T(8,128)S(1)}, u32[]{:S(2)}, u32[]{:S(2)}) %collective-permute-start.62) | collective-permute-done | bytes 49184 | tf_op jit(solution)/shard_map/ppermute | solution.py:596
  301.5 2.8 adam.9
  304.3 2.6 adam.10
  306.9 7.1 %collective-permute-done.56.refs_2_ = bf16[2,96,1536]{2,1,0:T(8,128)(2,1)} collective-permute-done((bf16[2,96,1536]{2,1,0:T(8,128)(2,1)}, bf16[2,96,1536]{2,1,0:T(8,128)(2,1)}, u32[]{:S(2)}, u32[]{:S(2)}) %collective-permute-start.56) | collective-permute-done | bytes 589856 | tf_op jit(solution)/shard_map/ppermute | solution.py:596
  314.0 5.1 %adam.11 = (f32[192,3072]{1,0:T(8,128)}, f32[192,3072]{1,0:T(8,128)}, f32[192,3072]{1,0:T(8,128)S(1)}, f32[2,512]{1,0:T(2,128)S(1)}) custom-call(s32[3]{0:T(128)S(1)} %pad_add_fusion.refs_0_, bf16[2,96,1536]{2,1,0:T(8,128)(2,1)} %join.5.refs_3_.refs_1_, ...), custom_call_target="tpu_custom_call", output_to_operand_aliasing={{0}: (6, {}), {1}: (7, {}), {2}: (8, {})} | custom-call | flops 999999995904 | bytes 10000000000 | tf_op jit(solution)/shard_map/adam/pallas_call | solution.py:50
  319.2 4.6 %adam.12 = (f32[192,3072]{1,0:T(8,128)}, f32[192,3072]{1,0:T(8,128)}, f32[192,3072]{1,0:T(8,128)S(1)}, f32[2,512]{1,0:T(2,128)S(1)}) custom-call(s32[3]{0:T(128)S(1)} %pad_add_fusion.refs_0_, bf16[2,96,1536]{2,1,0:T(8,128)(2,1)} %join.5.refs_3_.refs_1_, ...), custom_call_target="tpu_custom_call", output_to_operand_aliasing={{0}: (6, {}), {1}: (7, {}), {2}: (8, {})} | custom-call | flops 999999995904 | bytes 10000000000 | tf_op jit(solution)/shard_map/adam/pallas_call | solution.py:50
  323.9 5.1 %adam.13 = (f32[192,2304]{1,0:T(8,128)}, f32[192,2304]{1,0:T(8,128)}, f32[192,2304]{1,0:T(8,128)S(1)}, f32[2,256]{1,0:T(2,128)S(1)}) custom-call(s32[3]{0:T(128)S(1)} %pad_add_fusion.refs_0_, bf16[2,96,768]{2,1,0:T(8,128)(2,1)} %join.7.refs_6_.refs_1_, ...), custom_call_target="tpu_custom_call", output_to_operand_aliasing={{0}: (6, {}), {1}: (7, {}), {2}: (8, {})} | custom-call | flops 999999995904 | bytes 10000000000 | tf_op jit(solution)/shard_map/adam/pallas_call | solution.py:50
  333.0 1.9 vector_step.1
  337.9 4.2 %apply.1 = (f32[192,2304]{1,0:T(8,128)}, f32[192,768]{1,0:T(8,128)}, f32[192,3072]{1,0:T(8,128)}, f32[192,3072]{1,0:T(8,128)}, f32[8,128]{1,0:T(8,128)S(1)}) custom-call(f32[8,128]{1,0:T(8,128)} %add.15.refs_0_, f32[8,128]{1,0:T(8,128)} %collective-permute-done.58.refs_1_, f32[192,2304]{1,0:T(8,128)S(1)} %copy-done.39, f32[192,768]{1,0:T(8,128)S(1)} %bitcast.46, ...), custom_call_target="tpu_custom_call" | custom-call | flops 999999995904 | bytes 10000000000 | tf_op jit(solution)/shard_map/apply/pallas_call | solution.py:50
  (365 shorter events, 95.1 us)
Async XLA Ops:
  7.5 10.1 %collective-permute-start.4 = (bf16[192,768]{1,0:T(8,128)(2,1)}, bf16[192,768]{1,0:T(8,128)(2,1)}, u32[]{:S(2)}, u32[]{:S(2)}) collective-permute-start(bf16[192,768]{1,0:T(8,128)(2,1)} %get-tuple-element.131.refs_4_.refs_16_), channel_id=1, source_target_pairs={{0,2},{1,3},{2,0},{3,1},{4,6},{5,7},{6,4},{7,5},{8,10},{9,11},{10,... | collective-permute-start | bytes 884744 | tf_op jit(solution)/shard_map/ppermute | solution.py:596
  7.5 18.4 %collective-permute-start.3 = (bf16[192,768]{1,0:T(8,128)(2,1)}, bf16[192,768]{1,0:T(8,128)(2,1)}, u32[]{:S(2)}, u32[]{:S(2)}) collective-permute-start(bf16[192,768]{1,0:T(8,128)(2,1)} %get-tuple-element.131.refs_4_.refs_16_), channel_id=1, source_target_pairs={{0,1},{1,0},{2,3},{3,2},{4,5},{5,4},{6,7},{7,6},{8,9},{9,8},{10,11... | collective-permute-start | bytes 884744 | tf_op jit(solution)/shard_map/ppermute | solution.py:596
  8.0 18.4 %collective-permute-start.7 = (bf16[192,768]{1,0:T(8,128)(2,1)}, bf16[192,768]{1,0:T(8,128)(2,1)}, u32[]{:S(2)}, u32[]{:S(2)}) collective-permute-start(bf16[192,768]{1,0:T(8,128)(2,1)} %get-tuple-element.133.refs_4_.refs_20_), channel_id=1, source_target_pairs={{0,2},{1,3},{2,0},{3,1},{4,6},{5,7},{6,4},{7,5},{8,10},{9,11},{10,... | collective-permute-start | bytes 884744 | tf_op jit(solution)/shard_map/ppermute | solution.py:596
  14.2 19.3 %collective-permute-start.6 = (bf16[192,768]{1,0:T(8,128)(2,1)}, bf16[192,768]{1,0:T(8,128)(2,1)}, u32[]{:S(2)}, u32[]{:S(2)}) collective-permute-start(bf16[192,768]{1,0:T(8,128)(2,1)} %get-tuple-element.133.refs_4_.refs_20_), channel_id=1, source_target_pairs={{0,1},{1,0},{2,3},{3,2},{4,5},{5,4},{6,7},{7,6},{8,9},{9,8},{10,11... | collective-permute-start | bytes 884744 | tf_op jit(solution)/shard_map/ppermute | solution.py:596
  14.7 19.2 %collective-permute-start.10 = (bf16[192,768]{1,0:T(8,128)(2,1)}, bf16[192,768]{1,0:T(8,128)(2,1)}, u32[]{:S(2)}, u32[]{:S(2)}) collective-permute-start(bf16[192,768]{1,0:T(8,128)(2,1)} %get-tuple-element.135.refs_4_.refs_24_), channel_id=1, source_target_pairs={{0,2},{1,3},{2,0},{3,1},{4,6},{5,7},{6,4},{7,5},{8,10},{9,11},{10,... | collective-permute-start | bytes 884744 | tf_op jit(solution)/shard_map/ppermute | solution.py:596
  25.8 19.4 %collective-permute-start.9 = (bf16[192,768]{1,0:T(8,128)(2,1)}, bf16[192,768]{1,0:T(8,128)(2,1)}, u32[]{:S(2)}, u32[]{:S(2)}) collective-permute-start(bf16[192,768]{1,0:T(8,128)(2,1)} %get-tuple-element.135.refs_4_.refs_24_), channel_id=1, source_target_pairs={{0,1},{1,0},{2,3},{3,2},{4,5},{5,4},{6,7},{7,6},{8,9},{9,8},{10,11... | collective-permute-start | bytes 884744 | tf_op jit(solution)/shard_map/ppermute | solution.py:596
  26.4 18.8 %collective-permute-start.14 = (bf16[192,768]{1,0:T(8,128)(2,1)}, bf16[192,768]{1,0:T(8,128)(2,1)}, u32[]{:S(2)}, u32[]{:S(2)}) collective-permute-start(bf16[192,768]{1,0:T(8,128)(2,1)} %get-tuple-element.138.refs_6_.refs_8_), channel_id=1, source_target_pairs={{0,2},{1,3},{2,0},{3,1},{4,6},{5,7},{6,4},{7,5},{8,10},{9,11},{10,... | collective-permute-start | bytes 884744 | tf_op jit(solution)/shard_map/ppermute | solution.py:596
  26.5 9.4 %collective-permute-start.8 = (bf16[192,768]{1,0:T(8,128)(2,1)}, bf16[192,768]{1,0:T(8,128)(2,1)}, u32[]{:S(2)}, u32[]{:S(2)}) collective-permute-start(bf16[192,768]{1,0:T(8,128)(2,1)} %collective-permute-done.7.refs_6_.refs_22_), channel_id=1, source_target_pairs={{0,1},{1,0},{2,3},{3,2},{4,5},{5,4},{6,7},{7,6},{8,9},{9,8},{10,11... | collective-permute-start | bytes 884744 | tf_op jit(solution)/shard_map/ppermute | solution.py:596
  33.5 23.9 %collective-permute-start.13 = (bf16[192,768]{1,0:T(8,128)(2,1)}, bf16[192,768]{1,0:T(8,128)(2,1)}, u32[]{:S(2)}, u32[]{:S(2)}) collective-permute-start(bf16[192,768]{1,0:T(8,128)(2,1)} %get-tuple-element.138.refs_6_.refs_8_), channel_id=1, source_target_pairs={{0,1},{1,0},{2,3},{3,2},{4,5},{5,4},{6,7},{7,6},{8,9},{9,8},{10,11... | collective-permute-start | bytes 884744 | tf_op jit(solution)/shard_map/ppermute | solution.py:596
  34.0 9.5 %collective-permute-start.12 = (bf16[96,1536]{1,0:T(8,128)(2,1)}, bf16[96,1536]{1,0:T(8,128)(2,1)}, u32[]{:S(2)}, u32[]{:S(2)}) collective-permute-start(bf16[96,1536]{1,0:T(8,128)(2,1)} %get-tuple-element.136), channel_id=1, source_target_pairs={{0,2},{1,3},{2,0},{3,1},{4,6},{5,7},{6,4},{7,5},{8,10},{9,11},{10,... | collective-permute-start | bytes 884744 | tf_op jit(solution)/shard_map/ppermute | solution.py:596
  43.5 11.8 %collective-permute-start.16 = (bf16[96,1536]{1,0:T(8,128)(2,1)}, bf16[96,1536]{1,0:T(8,128)(2,1)}, u32[]{:S(2)}, u32[]{:S(2)}) collective-permute-start(bf16[96,1536]{1,0:T(8,128)(2,1)} %get-tuple-element.139), channel_id=1, source_target_pairs={{0,2},{1,3},{2,0},{3,1},{4,6},{5,7},{6,4},{7,5},{8,10},{9,11},{10,... | collective-permute-start | bytes 884744 | tf_op jit(solution)/shard_map/ppermute | solution.py:596
  45.2 12.6 %collective-permute-start.15 = (bf16[192,768]{1,0:T(8,128)(2,1)}, bf16[192,768]{1,0:T(8,128)(2,1)}, u32[]{:S(2)}, u32[]{:S(2)}) collective-permute-start(bf16[192,768]{1,0:T(8,128)(2,1)} %collective-permute-done.14.refs_8_.refs_10_), channel_id=1, source_target_pairs={{0,1},{1,0},{2,3},{3,2},{4,5},{5,4},{6,7},{7,6},{8,9},{9,8},{10,11... | collective-permute-start | bytes 884744 | tf_op jit(solution)/shard_map/ppermute | solution.py:596
  55.3 10.1 %collective-permute-start.21 = (bf16[96,1536]{1,0:T(8,128)(2,1)}, bf16[96,1536]{1,0:T(8,128)(2,1)}, u32[]{:S(2)}, u32[]{:S(2)}) collective-permute-start(bf16[96,1536]{1,0:T(8,128)(2,1)} %tie.4.refs_10_.refs_13_.refs_5_), channel_id=1, source_target_pairs={{0,4},{4,0},{8,12},{12,8},{16,20},{20,16},{24,28},{28,24},{1,5},{5... | collective-permute-start | bytes 884744 | tf_op jit(solution)/shard_map/ppermute | solution.py:596
  56.8 14.6 %collective-permute-start.18 = (bf16[96,1536]{1,0:T(8,128)(2,1)}, bf16[96,1536]{1,0:T(8,128)(2,1)}, u32[]{:S(2)}, u32[]{:S(2)}) collective-permute-start(bf16[96,1536]{1,0:T(8,128)(2,1)} %tie.3.refs_9_.refs_7_), channel_id=1, source_target_pairs={{0,4},{4,0},{8,12},{12,8},{16,20},{20,16},{24,28},{28,24},{1,5},{5... | collective-permute-start | bytes 884744 | tf_op jit(solution)/shard_map/ppermute | solution.py:596
  57.3 21.2 %collective-permute-start.17 = (bf16[192,3072]{1,0:T(8,128)(2,1)}, bf16[192,3072]{1,0:T(8,128)(2,1)}, u32[]{:S(2)}, u32[]{:S(2)}) collective-permute-start(bf16[192,3072]{1,0:T(8,128)(2,1)} %get-tuple-element.145.refs_5_.refs_11_.refs_3_), channel_id=1, source_target_pairs={{0,1},{1,0},{2,3},{3,2},{4,5},{5,4},{6,7},{7,6},{8,9},{9,8},{10,11... | collective-permute-start | bytes 3538952 | tf_op jit(solution)/shard_map/ppermute | solution.py:596
  57.3 20.5 %collective-permute-start.22 = (bf16[96,1536]{1,0:T(8,128)(2,1)}, bf16[96,1536]{1,0:T(8,128)(2,1)}, u32[]{:S(2)}, u32[]{:S(2)}) collective-permute-start(bf16[96,1536]{1,0:T(8,128)(2,1)} %tie.4.refs_10_.refs_13_.refs_5_), channel_id=1, source_target_pairs={{0,1},{1,0},{2,3},{3,2},{4,5},{5,4},{6,7},{7,6},{8,9},{9,8},{10,11... | collective-permute-start | bytes 884744 | tf_op jit(solution)/shard_map/ppermute | solution.py:596
  57.9 20.3 %collective-permute-start.19 = (bf16[96,1536]{1,0:T(8,128)(2,1)}, bf16[96,1536]{1,0:T(8,128)(2,1)}, u32[]{:S(2)}, u32[]{:S(2)}) collective-permute-start(bf16[96,1536]{1,0:T(8,128)(2,1)} %tie.3.refs_9_.refs_7_), channel_id=1, source_target_pairs={{0,1},{1,0},{2,3},{3,2},{4,5},{5,4},{6,7},{7,6},{8,9},{9,8},{10,11... | collective-permute-start | bytes 884744 | tf_op jit(solution)/shard_map/ppermute | solution.py:596
  65.4 13.1 %collective-permute-start.23 = (bf16[96,1536]{1,0:T(8,128)(2,1)}, bf16[96,1536]{1,0:T(8,128)(2,1)}, u32[]{:S(2)}, u32[]{:S(2)}) collective-permute-start(bf16[96,1536]{1,0:T(8,128)(2,1)} %collective-permute-done.21.refs_14_.refs_6_), channel_id=1, source_target_pairs={{0,1},{1,0},{2,3},{3,2},{4,5},{5,4},{6,7},{7,6},{8,9},{9,8},{10,11... | collective-permute-start | bytes 884744 | tf_op jit(solution)/shard_map/ppermute | solution.py:596
  77.8 31.9 %collective-permute-start.25 = (bf16[192,3072]{1,0:T(8,128)(2,1)}, bf16[192,3072]{1,0:T(8,128)(2,1)}, u32[]{:S(2)}, u32[]{:S(2)}) collective-permute-start(bf16[192,3072]{1,0:T(8,128)(2,1)} %get-tuple-element.147.refs_5_.refs_9_.refs_3_), channel_id=1, source_target_pairs={{0,2},{1,3},{2,0},{3,1},{4,6},{5,7},{6,4},{7,5},{8,10},{9,11},{10,... | collective-permute-start | bytes 3538952 | tf_op jit(solution)/shard_map/ppermute | solution.py:596
  78.2 39.6 %collective-permute-start.24 = (bf16[192,3072]{1,0:T(8,128)(2,1)}, bf16[192,3072]{1,0:T(8,128)(2,1)}, u32[]{:S(2)}, u32[]{:S(2)}) collective-permute-start(bf16[192,3072]{1,0:T(8,128)(2,1)} %get-tuple-element.147.refs_5_.refs_9_.refs_3_), channel_id=1, source_target_pairs={{0,1},{1,0},{2,3},{3,2},{4,5},{5,4},{6,7},{7,6},{8,9},{9,8},{10,11... | collective-permute-start | bytes 3538952 | tf_op jit(solution)/shard_map/ppermute | solution.py:596
  99.5 10.8 %collective-permute-start.27 = (bf16[2,2,192,1536]{3,2,1,0:T(8,128)(2,1)}, bf16[2,2,192,1536]{3,2,1,0:T(8,128)(2,1)}, u32[]{:S(2)}, u32[]{:S(2)}) collective-permute-start(bf16[2,2,192,1536]{3,2,1,0:T(8,128)(2,1)} %bitcast.7), channel_id=1, source_target_pairs={{0,1},{1,0},{2,3},{3,2},{4,5},{5,4},{6,7},{7,6},{8,9},{9,8},{10,11... | collective-permute-start | bytes 7077896 | tf_op jit(solution)/shard_map/ppermute | solution.py:596
  116.3 36.1 %collective-permute-start.29 = (bf16[2,192,1536]{2,1,0:T(8,128)(2,1)}, bf16[2,192,1536]{2,1,0:T(8,128)(2,1)}, u32[]{:S(2)}, u32[]{:S(2)}) collective-permute-start(bf16[2,192,1536]{2,1,0:T(8,128)(2,1)} %far.4.refs_15_), channel_id=1, source_target_pairs={{0,2},{1,3},{2,0},{3,1},{4,6},{5,7},{6,4},{7,5},{8,10},{9,11},{10,... | collective-permute-start | bytes 3538952 | tf_op jit(solution)/shard_map/ppermute | solution.py:596
  155.7 18.9 %collective-permute-start.30 = (bf16[2,96,1536]{2,1,0:T(8,128)(2,1)}, bf16[2,96,1536]{2,1,0:T(8,128)(2,1)}, u32[]{:S(2)}, u32[]{:S(2)}) collective-permute-start(bf16[2,96,1536]{2,1,0:T(8,128)(2,1)} %get-tuple-element.156.refs_13_), channel_id=1, source_target_pairs={{0,4},{4,0},{8,12},{12,8},{16,20},{20,16},{24,28},{28,24},{1,5},{5... | collective-permute-start | bytes 1769480 | tf_op jit(solution)/shard_map/ppermute | solution.py:596
  173.4 29.1 %collective-permute-start.35 = (bf16[2,192,1536]{2,1,0:T(8,128)(2,1)}, bf16[2,192,1536]{2,1,0:T(8,128)(2,1)}, u32[]{:S(2)}, u32[]{:S(2)}) collective-permute-start(bf16[2,192,1536]{2,1,0:T(8,128)(2,1)} %far.5.refs_4_.refs_12_), channel_id=1, source_target_pairs={{0,2},{1,3},{2,0},{3,1},{4,6},{5,7},{6,4},{7,5},{8,10},{9,11},{10,... | collective-permute-start | bytes 3538952 | tf_op jit(solution)/shard_map/ppermute | solution.py:596
  176.5 11.4 %collective-permute-start.33 = (bf16[2,48,1536]{2,1,0:T(8,128)(2,1)}, bf16[2,48,1536]{2,1,0:T(8,128)(2,1)}, u32[]{:S(2)}, u32[]{:S(2)}) collective-permute-start(bf16[2,48,1536]{2,1,0:T(8,128)(2,1)} %get-tuple-element.165.refs_5_), channel_id=1, source_target_pairs={{0,8},{4,12},{8,0},{12,4},{16,24},{20,28},{24,16},{28,20},{1,9},{5... | collective-permute-start | bytes 884744 | tf_op jit(solution)/shard_map/ppermute | solution.py:596
  187.8 28.1 %collective-permute-start.37 = (bf16[1,2,192,768]{3,2,1,0:T(8,128)(2,1)}, bf16[1,2,192,768]{3,2,1,0:T(8,128)(2,1)}, u32[]{:S(2)}, u32[]{:S(2)}) collective-permute-start(bf16[1,2,192,768]{3,2,1,0:T(8,128)(2,1)} %bitcast.15), channel_id=1, source_target_pairs={{0,1},{1,0},{2,3},{3,2},{4,5},{5,4},{6,7},{7,6},{8,9},{9,8},{10,11... | collective-permute-start | bytes 1769480 | tf_op jit(solution)/shard_map/ppermute | solution.py:596
  197.4 18.5 %collective-permute-start.38 = (bf16[1,2,192,768]{3,2,1,0:T(8,128)(2,1)S(1)}, bf16[1,2,192,768]{3,2,1,0:T(8,128)(2,1)S(1)}, u32[]{:S(2)}, u32[]{:S(2)}) collective-permute-start(bf16[1,2,192,768]{3,2,1,0:T(8,128)(2,1)S(1)} %bitcast.48), channel_id=1, source_target_pairs={{0,1},{1,0},{2,3},{3,2},{4,5},{5,4},{6,7},{7,6},{8,9},{9,8},{10,11... | collective-permute-start | bytes 1769480 | tf_op jit(solution)/shard_map/ppermute | solution.py:596
  197.5 22.0 %collective-permute-start.36 = (bf16[2,192,768]{2,1,0:T(8,128)(2,1)S(1)}, bf16[2,192,768]{2,1,0:T(8,128)(2,1)S(1)}, u32[]{:S(2)}, u32[]{:S(2)}) collective-permute-start(bf16[2,192,768]{2,1,0:T(8,128)(2,1)S(1)} %far.6.refs_6_), channel_id=1, source_target_pairs={{0,2},{1,3},{2,0},{3,1},{4,6},{5,7},{6,4},{7,5},{8,10},{9,11},{10,... | collective-permute-start | bytes 1769480 | tf_op jit(solution)/shard_map/ppermute | solution.py:596
  198.4 16.2 %collective-permute-start.34 = (bf16[2,48,1536]{2,1,0:T(8,128)(2,1)S(1)}, bf16[2,48,1536]{2,1,0:T(8,128)(2,1)S(1)}, u32[]{:S(2)}, u32[]{:S(2)}) collective-permute-start(bf16[2,48,1536]{2,1,0:T(8,128)(2,1)S(1)} %rest.4.refs_5_.refs_1_), channel_id=1, source_target_pairs={{0,16},{4,20},{8,24},{12,28},{16,0},{20,4},{24,8},{28,12},{1,17},{... | collective-permute-start | bytes 884744 | tf_op jit(solution)/shard_map/ppermute | solution.py:596
  205.7 29.4 %collective-permute-start.41 = (bf16[2,96,1536]{2,1,0:T(8,128)(2,1)}, bf16[2,96,1536]{2,1,0:T(8,128)(2,1)}, u32[]{:S(2)}, u32[]{:S(2)}) collective-permute-start(bf16[2,96,1536]{2,1,0:T(8,128)(2,1)} %get-tuple-element.184.refs_3_.refs_29_), channel_id=1, source_target_pairs={{0,4},{4,0},{8,12},{12,8},{16,20},{20,16},{24,28},{28,24},{1,5},{5... | collective-permute-start | bytes 1769480 | tf_op jit(solution)/shard_map/ppermute | solution.py:596
  215.9 14.6 %collective-permute-start.42 = (bf16[2,48,1536]{2,1,0:T(8,128)(2,1)}, bf16[2,48,1536]{2,1,0:T(8,128)(2,1)}, u32[]{:S(2)}, u32[]{:S(2)}) collective-permute-start(bf16[2,48,1536]{2,1,0:T(8,128)(2,1)} %part.4.refs_5_.refs_28_.refs_1_), channel_id=1, source_target_pairs={{0,8},{4,12},{8,0},{12,4},{16,24},{20,28},{24,16},{28,20},{1,9},{5... | collective-permute-start | bytes 884744 | tf_op jit(solution)/shard_map/ppermute | solution.py:596
  218.3 20.1 %collective-permute-start.40 = (bf16[2,192,768]{2,1,0:T(8,128)(2,1)}, bf16[2,192,768]{2,1,0:T(8,128)(2,1)}, u32[]{:S(2)}, u32[]{:S(2)}) collective-permute-start(bf16[2,192,768]{2,1,0:T(8,128)(2,1)} %far.7.refs_6_.refs_31_), channel_id=1, source_target_pairs={{0,2},{1,3},{2,0},{3,1},{4,6},{5,7},{6,4},{7,5},{8,10},{9,11},{10,... | collective-permute-start | bytes 1769480 | tf_op jit(solution)/shard_map/ppermute | solution.py:596
  221.0 19.5 %collective-permute-start.39 = (bf16[2,96,768]{2,1,0:T(8,128)(2,1)}, bf16[2,96,768]{2,1,0:T(8,128)(2,1)}, u32[]{:S(2)}, u32[]{:S(2)}) collective-permute-start(bf16[2,96,768]{2,1,0:T(8,128)(2,1)} %get-tuple-element.189.refs_30_), channel_id=1, source_target_pairs={{0,4},{4,0},{8,12},{12,8},{16,20},{20,16},{24,28},{28,24},{1,5},{5... | collective-permute-start | bytes 884744 | tf_op jit(solution)/shard_map/ppermute | solution.py:596
  233.5 26.1 %collective-permute-start.49 = (bf16[2,96,1536]{2,1,0:T(8,128)(2,1)S(1)}, bf16[2,96,1536]{2,1,0:T(8,128)(2,1)S(1)}, u32[]{:S(2)}, u32[]{:S(2)}) collective-permute-start(bf16[2,96,1536]{2,1,0:T(8,128)(2,1)S(1)} %join.4.refs_3_.refs_1_), channel_id=1, source_target_pairs={{0,4},{4,0},{8,12},{12,8},{16,20},{20,16},{24,28},{28,24},{1,5},{5... | collective-permute-start | bytes 1769480 | tf_op jit(solution)/shard_map/ppermute | solution.py:596
  236.3 9.8 %collective-permute-start.45 = (bf16[2,48,1536]{2,1,0:T(8,128)(2,1)S(1)}, bf16[2,48,1536]{2,1,0:T(8,128)(2,1)S(1)}, u32[]{:S(2)}, u32[]{:S(2)}) collective-permute-start(bf16[2,48,1536]{2,1,0:T(8,128)(2,1)S(1)} %get-tuple-element.193.refs_6_), channel_id=1, source_target_pairs={{0,8},{4,12},{8,0},{12,4},{16,24},{20,28},{24,16},{28,20},{1,9},{5... | collective-permute-start | bytes 884744 | tf_op jit(solution)/shard_map/ppermute | solution.py:596
  239.9 14.8 %collective-permute-start.44 = (bf16[2,96,768]{2,1,0:T(8,128)(2,1)S(1)}, bf16[2,96,768]{2,1,0:T(8,128)(2,1)S(1)}, u32[]{:S(2)}, u32[]{:S(2)}) collective-permute-start(bf16[2,96,768]{2,1,0:T(8,128)(2,1)S(1)} %get-tuple-element.194.refs_3_), channel_id=1, source_target_pairs={{0,4},{4,0},{8,12},{12,8},{16,20},{20,16},{24,28},{28,24},{1,5},{5... | collective-permute-start | bytes 884744 | tf_op jit(solution)/shard_map/ppermute | solution.py:596
  241.5 16.1 %collective-permute-start.43 = (bf16[2,48,768]{2,1,0:T(8,128)(2,1)S(1)}, bf16[2,48,768]{2,1,0:T(8,128)(2,1)S(1)}, u32[]{:S(2)}, u32[]{:S(2)}) collective-permute-start(bf16[2,48,768]{2,1,0:T(8,128)(2,1)S(1)} %get-tuple-element.196.refs_3_), channel_id=1, source_target_pairs={{0,8},{4,12},{8,0},{12,4},{16,24},{20,28},{24,16},{28,20},{1,9},{5... | collective-permute-start | bytes 442376 | tf_op jit(solution)/shard_map/ppermute | solution.py:596
  247.4 15.5 %collective-permute-start.48 = (bf16[2,48,1536]{2,1,0:T(8,128)(2,1)}, bf16[2,48,1536]{2,1,0:T(8,128)(2,1)}, u32[]{:S(2)}, u32[]{:S(2)}) collective-permute-start(bf16[2,48,1536]{2,1,0:T(8,128)(2,1)} %rest.5.refs_3_.refs_1_), channel_id=1, source_target_pairs={{0,16},{4,20},{8,24},{12,28},{16,0},{20,4},{24,8},{28,12},{1,17},{... | collective-permute-start | bytes 884744 | tf_op jit(solution)/shard_map/ppermute | solution.py:596
  255.9 10.6 %collective-permute-start.47 = (bf16[2,48,768]{2,1,0:T(8,128)(2,1)}, bf16[2,48,768]{2,1,0:T(8,128)(2,1)}, u32[]{:S(2)}, u32[]{:S(2)}) collective-permute-start(bf16[2,48,768]{2,1,0:T(8,128)(2,1)} %get-tuple-element.199.refs_3_), channel_id=1, source_target_pairs={{0,8},{4,12},{8,0},{12,4},{16,24},{20,28},{24,16},{28,20},{1,9},{5... | collective-permute-start | bytes 442376 | tf_op jit(solution)/shard_map/ppermute | solution.py:596
  258.9 10.1 %collective-permute-start.46 = (bf16[2,48,768]{2,1,0:T(8,128)(2,1)}, bf16[2,48,768]{2,1,0:T(8,128)(2,1)}, u32[]{:S(2)}, u32[]{:S(2)}) collective-permute-start(bf16[2,48,768]{2,1,0:T(8,128)(2,1)} %rest.6.refs_6_.refs_1_), channel_id=1, source_target_pairs={{0,16},{4,20},{8,24},{12,28},{16,0},{20,4},{24,8},{28,12},{1,17},{... | collective-permute-start | bytes 442376 | tf_op jit(solution)/shard_map/ppermute | solution.py:596
  264.7 13.2 %collective-permute-start.52 = (bf16[2,48,1536]{2,1,0:T(8,128)(2,1)}, bf16[2,48,1536]{2,1,0:T(8,128)(2,1)}, u32[]{:S(2)}, u32[]{:S(2)}) collective-permute-start(bf16[2,48,1536]{2,1,0:T(8,128)(2,1)} %part.5.refs_3_.refs_1_), channel_id=1, source_target_pairs={{0,8},{4,12},{8,0},{12,4},{16,24},{20,28},{24,16},{28,20},{1,9},{5... | collective-permute-start | bytes 884744 | tf_op jit(solution)/shard_map/ppermute | solution.py:596
  268.2 11.6 %collective-permute-start.51 = (bf16[2,48,768]{2,1,0:T(8,128)(2,1)}, bf16[2,48,768]{2,1,0:T(8,128)(2,1)}, u32[]{:S(2)}, u32[]{:S(2)}) collective-permute-start(bf16[2,48,768]{2,1,0:T(8,128)(2,1)} %rest.7.refs_3_.refs_1_), channel_id=1, source_target_pairs={{0,16},{4,20},{8,24},{12,28},{16,0},{20,4},{24,8},{28,12},{1,17},{... | collective-permute-start | bytes 442376 | tf_op jit(solution)/shard_map/ppermute | solution.py:596
  270.7 10.2 %collective-permute-start.50 = (bf16[2,48,768]{2,1,0:T(8,128)(2,1)}, bf16[2,48,768]{2,1,0:T(8,128)(2,1)}, u32[]{:S(2)}, u32[]{:S(2)}) collective-permute-start(bf16[2,48,768]{2,1,0:T(8,128)(2,1)} %part.6.refs_6_.refs_1_), channel_id=1, source_target_pairs={{0,8},{4,12},{8,0},{12,4},{16,24},{20,28},{24,16},{28,20},{1,9},{5... | collective-permute-start | bytes 442376 | tf_op jit(solution)/shard_map/ppermute | solution.py:596
  281.9 19.6 %collective-permute-start.53 = (bf16[2,96,768]{2,1,0:T(8,128)(2,1)S(1)}, bf16[2,96,768]{2,1,0:T(8,128)(2,1)S(1)}, u32[]{:S(2)}, u32[]{:S(2)}) collective-permute-start(bf16[2,96,768]{2,1,0:T(8,128)(2,1)S(1)} %join.6.refs_3_.refs_1_), channel_id=1, source_target_pairs={{0,4},{4,0},{8,12},{12,8},{16,20},{20,16},{24,28},{28,24},{1,5},{5... | collective-permute-start | bytes 884744 | tf_op jit(solution)/shard_map/ppermute | solution.py:596
  285.3 13.5 %collective-permute-start.54 = (bf16[2,48,768]{2,1,0:T(8,128)(2,1)S(1)}, bf16[2,48,768]{2,1,0:T(8,128)(2,1)S(1)}, u32[]{:S(2)}, u32[]{:S(2)}) collective-permute-start(bf16[2,48,768]{2,1,0:T(8,128)(2,1)S(1)} %part.7.refs_3_.refs_1_), channel_id=1, source_target_pairs={{0,8},{4,12},{8,0},{12,4},{16,24},{20,28},{24,16},{28,20},{1,9},{5... | collective-permute-start | bytes 442376 | tf_op jit(solution)/shard_map/ppermute | solution.py:596
  297.5 35.4 %collective-permute-start.63 = (f32[16,768]{1,0:T(8,128)}, f32[16,768]{1,0:T(8,128)}, u32[]{:S(2)}, u32[]{:S(2)}) collective-permute-start(f32[16,768]{1,0:T(8,128)} %add.19.refs_1_), channel_id=1, source_target_pairs={{0,16},{4,20},{8,24},{12,28},{16,0},{20,4},{24,8},{28,12},{1,17},{... | collective-permute-start | bytes 147464 | tf_op jit(solution)/shard_map/ppermute | solution.py:596
  298.2 15.8 %collective-permute-start.56 = (bf16[2,96,1536]{2,1,0:T(8,128)(2,1)}, bf16[2,96,1536]{2,1,0:T(8,128)(2,1)}, u32[]{:S(2)}, u32[]{:S(2)}) collective-permute-start(bf16[2,96,1536]{2,1,0:T(8,128)(2,1)} %join.5.refs_3_.refs_1_), channel_id=1, source_target_pairs={{0,4},{4,0},{8,12},{12,8},{16,20},{20,16},{24,28},{28,24},{1,5},{5... | collective-permute-start | bytes 1769480 | tf_op jit(solution)/shard_map/ppermute | solution.py:596
  300.0 23.8 %collective-permute-start.55 = (bf16[2,96,768]{2,1,0:T(8,128)(2,1)}, bf16[2,96,768]{2,1,0:T(8,128)(2,1)}, u32[]{:S(2)}, u32[]{:S(2)}) collective-permute-start(bf16[2,96,768]{2,1,0:T(8,128)(2,1)} %join.7.refs_6_.refs_1_), channel_id=1, source_target_pairs={{0,4},{4,0},{8,12},{12,8},{16,20},{20,16},{24,28},{28,24},{1,5},{5... | collective-permute-start | bytes 884744 | tf_op jit(solution)/shard_map/ppermute | solution.py:596
  (127 other events, 710.1 us)
